TPU v7x, 32 devices: a whole 2x2x4 slice. The times are simulated.
32 devices in a mesh: ctx: 32 (over z, y, x, core), tp: 1.
Axes of the slice: x: 2, y: 2, z: 4, core: 2. Of those that a mesh axis runs over, the one named last changes fastest.
Arguments:
- queries: bfloat16 [4096, 8192], P('ctx', 'tp'), may hold values from -32 to 32
- key_proj: bfloat16 [4096, 1024], P('ctx', 'tp'), may hold values from -12.5 to 12.5
- value_proj: bfloat16 [4096, 1024], P('ctx', 'tp'), may hold values from -6 to 6
- grad_out: bfloat16 [4096, 8192], P('ctx', 'tp'), may hold values from -6 to 6
- key_weight: bfloat16 [8192, 1024], P(None, 'tp'), may hold values from -0.1875 to 0.1875
- value_weight: bfloat16 [8192, 1024], P(None, 'tp'), may hold values from -0.1875 to 0.1875
- doc_start: int32 [4096], P('ctx'), may hold values from 0 to 4095, as said below
Outputs:
- grad_query: bfloat16 [4096, 8192], P('ctx', 'tp')
- grad_key: bfloat16 [4096, 1024], P('ctx', 'tp')
- grad_value: bfloat16 [4096, 1024], P('ctx', 'tp')
- grad_input: bfloat16 [4096, 8192], P('ctx', 'tp')
Inputs may be any that keep to these rules, and one draw needn't show every extreme that they name: doc_start[p] is the first position of the document holding p; documents are runs of consecutive positions, each of 1 to 2048 positions; the first document has exactly 2048 positions and the last position is a document of its own.
All inputs are finite; a program needn't handle non-finite values.
Results may differ from a plain program's by a relative error of at most 0.034.
Values may be sent and summed in bfloat16 or wider, within the bound.
A program may use at most 128 MiB of HBM per device.

v0:
```python
import functools
import math

import jax
import jax.numpy as jnp
from jax import lax
from jax.experimental import pallas as pl
from jax.experimental.pallas import tpu as pltpu
from jax.sharding import PartitionSpec as P

HEADS = 64
KV_HEADS = 8
HD = 128
GROUP = HEADS // KV_HEADS
DOC_MOST = 2048
TILE = 256
CHUNKS = 4

NEGATIVE = -1e30
NT = (((1,), (1,)), ((), ()))


def attention_kernel(
    tok_rows, key_tiles, marks, pos_ref, first_ref, query_ref, cot_ref, kv_ref, dq_ref, dkv_ref,
    query_rows, cot_rows, score_ref, weight_ref, dqt_ref,
):
    rows = GROUP * tok_rows
    soft_scale = 1.0 / math.sqrt(HD)
    exp2_scale = soft_scale * math.log2(math.e)
    low, full_low, full_high, high = marks[0], marks[1], marks[2], marks[3]

    for head in range(GROUP):
        query_rows[head * tok_rows:(head + 1) * tok_rows, :] = query_ref[:, head * HD:(head + 1) * HD]
        cot_rows[head * tok_rows:(head + 1) * tok_rows, :] = cot_ref[:, head * HD:(head + 1) * HD]

    def fold(values):
        return values.reshape(TILE // 8, 8, rows)

    def at(tile):
        return pl.ds(pl.multiple_of(tile * TILE, TILE), TILE)

    def slot(tile):
        return pl.ds(pl.multiple_of((tile - low) * TILE, TILE), TILE)

    def score_step(masked, tile, rowmax):
        scores = lax.dot_general(
            kv_ref[at(tile), :HD], query_rows[...], NT, preferred_element_type=jnp.float32
        )
        if masked:
            key_pos = tile * TILE + lax.broadcasted_iota(jnp.int32, (TILE, rows), 0)
            visible = (key_pos <= pos_ref[...]) & (key_pos >= first_ref[...])
            scores = jnp.where(visible, scores, NEGATIVE)
        score_ref[slot(tile), :] = scores
        return jnp.maximum(rowmax, jnp.max(fold(scores), axis=0))

    rowmax = jnp.full((8, rows), NEGATIVE, jnp.float32)
    rowmax = lax.fori_loop(low, full_low, functools.partial(score_step, True), rowmax)
    rowmax = lax.fori_loop(full_low, full_high, functools.partial(score_step, False), rowmax)
    rowmax = lax.fori_loop(full_high, high, functools.partial(score_step, True), rowmax)
    shift = jnp.max(rowmax, axis=0, keepdims=True) * exp2_scale

    def weight_step(tile, sums):
        total, dot_sum = sums
        weights = jnp.exp2(score_ref[slot(tile), :] * exp2_scale - shift)
        grad_probs = lax.dot_general(
            kv_ref[at(tile), HD:], cot_rows[...], NT, preferred_element_type=jnp.float32
        )
        weight_ref[slot(tile), :] = weights.astype(jnp.bfloat16)
        score_ref[slot(tile), :] = grad_probs
        total = total + jnp.sum(fold(weights), axis=0)
        dot_sum = dot_sum + jnp.sum(fold(weights * grad_probs), axis=0)
        return (total, dot_sum)

    zeros = jnp.zeros((8, rows), jnp.float32)
    total, dot_sum = lax.fori_loop(low, high, weight_step, (zeros, zeros))
    inverse = 1.0 / jnp.sum(total, axis=0, keepdims=True)
    delta = jnp.sum(dot_sum, axis=0, keepdims=True) * inverse

    for head in range(GROUP):
        part = slice(head * tok_rows, (head + 1) * tok_rows)
        scale = jnp.broadcast_to(inverse[:, part], (HD, tok_rows)).T
        query_rows[part, :] = (query_rows[part, :].astype(jnp.float32) * (scale * soft_scale)).astype(jnp.bfloat16)
        cot_rows[part, :] = (cot_rows[part, :].astype(jnp.float32) * scale).astype(jnp.bfloat16)

    dqt_ref[...] = jnp.zeros_like(dqt_ref)

    def grad_step(tile, nothing):
        weights = weight_ref[slot(tile), :]
        grad_scores = (
            weights.astype(jnp.float32) * (score_ref[slot(tile), :] - delta)
        ).astype(jnp.bfloat16)
        dkv_ref[at(tile), HD:] = jnp.dot(
            weights, cot_rows[...], preferred_element_type=jnp.float32
        ).astype(jnp.bfloat16)
        dkv_ref[at(tile), :HD] = jnp.dot(
            grad_scores, query_rows[...], preferred_element_type=jnp.float32
        ).astype(jnp.bfloat16)
        dqt_ref[...] += jnp.dot(
            kv_ref[at(tile), :HD].T, grad_scores, preferred_element_type=jnp.float32
        )
        return nothing

    lax.fori_loop(low, high, grad_step, 0)

    def clear(tile, nothing):
        dkv_ref[at(tile), :] = jnp.zeros((TILE, 2 * HD), jnp.bfloat16)
        return nothing

    lax.fori_loop(0, low, clear, 0)
    lax.fori_loop(high, key_tiles, clear, 0)

    out_scale = inverse * soft_scale
    for head in range(GROUP):
        part = slice(head * tok_rows, (head + 1) * tok_rows)
        dq_ref[:, head * HD:(head + 1) * HD] = (dqt_ref[:, part] * out_scale[:, part]).T.astype(jnp.bfloat16)


def attention(marks, pos, first, queries, grad_out, kv, tok_rows, first_head, heads_here):
    rows = GROUP * tok_rows
    keys = kv.shape[0]
    slots = (DOC_MOST + tok_rows + 2 * TILE - 2) // TILE * TILE
    wide = GROUP * HD
    flops = heads_here * 5 * 2 * rows * (DOC_MOST // 2) * HD
    return pl.pallas_call(
        functools.partial(attention_kernel, tok_rows, keys // TILE),
        grid_spec=pltpu.PrefetchScalarGridSpec(
            num_scalar_prefetch=1,
            grid=(heads_here,),
            in_specs=[
                pl.BlockSpec((1, rows), lambda h, marks: (0, 0)),
                pl.BlockSpec((1, rows), lambda h, marks: (0, 0)),
                pl.BlockSpec((tok_rows, wide), lambda h, marks: (0, first_head + h)),
                pl.BlockSpec((tok_rows, wide), lambda h, marks: (0, first_head + h)),
                pl.BlockSpec((keys, 2 * HD), lambda h, marks: (0, h)),
            ],
            out_specs=[
                pl.BlockSpec((tok_rows, wide), lambda h, marks: (0, h)),
                pl.BlockSpec((keys, 2 * HD), lambda h, marks: (0, h)),
            ],
            scratch_shapes=[
                pltpu.VMEM((rows, HD), jnp.bfloat16),
                pltpu.VMEM((rows, HD), jnp.bfloat16),
                pltpu.VMEM((slots, rows), jnp.float32),
                pltpu.VMEM((slots, rows), jnp.bfloat16),
                pltpu.VMEM((HD, rows), jnp.float32),
            ],
        ),
        out_shape=[
            jax.ShapeDtypeStruct((tok_rows, heads_here * wide), jnp.bfloat16),
            jax.ShapeDtypeStruct((keys, heads_here * 2 * HD), jnp.bfloat16),
        ],
        compiler_params=pltpu.CompilerParams(
            dimension_semantics=("arbitrary",), vmem_limit_bytes=48 * 1024 * 1024
        ),
        cost_estimate=pl.CostEstimate(flops=flops * 4, bytes_accessed=heads_here * 4 * 1024 * 1024, transcendentals=0),
    )(marks, pos, first, queries, grad_out, kv)


def shards(queries, key_proj, value_proj, grad_out, key_weight, value_weight, doc_start):
    tok_rows = queries.shape[0]
    heads_kv = key_proj.shape[1] // HD
    my_index = lax.axis_index("ctx")
    begin = my_index * tok_rows
    low = doc_start[0] // TILE
    full_low = (doc_start[tok_rows - 1] + TILE - 1) // TILE
    full_high = (begin + 1) // TILE
    high = (begin + tok_rows + TILE - 1) // TILE
    full_low = jnp.minimum(full_low, high)
    full_high = jnp.maximum(full_high, full_low)
    marks = jnp.stack([low, full_low, full_high, high]).astype(jnp.int32)
    pos = jnp.tile(begin + jnp.arange(tok_rows, dtype=jnp.int32), GROUP)[None]
    first = jnp.tile(doc_start, GROUP)[None]

    chunks = min(CHUNKS, heads_kv)
    per = heads_kv // chunks
    pair = jnp.stack(
        [key_proj.reshape(tok_rows, heads_kv, HD), value_proj.reshape(tok_rows, heads_kv, HD)], axis=2
    ).reshape(tok_rows, heads_kv * 2 * HD)
    grad_queries, sums = [], []
    for chunk in range(chunks):
        part = pair[:, chunk * per * 2 * HD:(chunk + 1) * per * 2 * HD]
        kv = lax.all_gather(part, "ctx", tiled=True)
        dq, dkv = attention(marks, pos, first, queries, grad_out, kv, tok_rows, chunk * per, per)
        grad_queries.append(dq)
        sums.append(lax.psum_scatter(dkv, "ctx", scatter_dimension=0, tiled=True))
    grad_query = jnp.concatenate(grad_queries, axis=1)
    both = jnp.concatenate(sums, axis=1).reshape(tok_rows, heads_kv, 2, HD)
    grad_key = both[:, :, 0].reshape(tok_rows, heads_kv * HD)
    grad_value = both[:, :, 1].reshape(tok_rows, heads_kv * HD)
    partial_input = jnp.einsum(
        "rc,dc->rd", grad_key, key_weight, preferred_element_type=jnp.float32
    )
    partial_input = partial_input + jnp.einsum(
        "rc,dc->rd", grad_value, value_weight, preferred_element_type=jnp.float32
    )
    grad_input = lax.psum_scatter(
        partial_input.astype(jnp.bfloat16), "tp", scatter_dimension=1, tiled=True
    )
    return (grad_query, grad_key, grad_value, grad_input)


def solution(mesh):
    in_specs = (
        P("ctx", "tp"),
        P("ctx", "tp"),
        P("ctx", "tp"),
        P("ctx", "tp"),
        P(None, "tp"),
        P(None, "tp"),
        P("ctx"),
    )
    out_specs = (P("ctx", "tp"), P("ctx", "tp"), P("ctx", "tp"), P("ctx", "tp"))
    return jax.shard_map(shards, mesh=mesh, in_specs=in_specs, out_specs=out_specs, check_vma=False)
```

profile of v0, /device:TPU:0, one launch (start us, length us, event | category | flops | bytes accessed | tf_op | source)
XLA Modules:
  0.0 867.2 jit_solution(16094670718787675191)
XLA Ops:
  9.5 1.2 pad_maximum_fusion.1
  17.7 59.1 %all-gather.5.cloned.1.call-done.kv_ref = bf16[4096,512]{1,0:T(8,128)(2,1)} async-done(((bf16[128,512]{1,0:T(8,128)(2,1)}), bf16[4096,512]{1,0:T(8,128)(2,1)}) %all-gather.5.cloned.1.call-update) | async-done | bytes 4194320 | tf_op jit(solution)/shard_map/all_gather | solution.py:182
  76.8 1.6 copy-done
  78.4 1.6 copy-done.4
  80.0 7.3 shard_map.102
  87.4 53.5 %all-gather.7.cloned.1.call-done.kv_ref = bf16[4096,512]{1,0:T(8,128)(2,1)} async-done(((bf16[128,512]{1,0:T(8,128)(2,1)}), bf16[4096,512]{1,0:T(8,128)(2,1)}) %all-gather.7.cloned.1.call-update) | async-done | bytes 4194320 | tf_op jit(solution)/shard_map/all_gather | solution.py:182
  140.9 1.6 copy-done.1
  142.5 1.6 copy-done.5
  144.0 7.3 shard_map.103
  151.4 53.5 %all-gather.9.cloned.1.call-done.kv_ref = bf16[4096,512]{1,0:T(8,128)(2,1)} async-done(((bf16[128,512]{1,0:T(8,128)(2,1)}), bf16[4096,512]{1,0:T(8,128)(2,1)}) %all-gather.9.cloned.1.call-update) | async-done | bytes 4194320 | tf_op jit(solution)/shard_map/all_gather | solution.py:182
  204.9 1.6 copy-done.2
  206.5 1.6 copy-done.6
  208.1 7.3 shard_map.104
  215.6 53.2 %all-gather.11.cloned.1.call-done.kv_ref = bf16[4096,512]{1,0:T(8,128)(2,1)} async-done(((bf16[128,512]{1,0:T(8,128)(2,1)}), bf16[4096,512]{1,0:T(8,128)(2,1)}) %all-gather.11.cloned.1.call-update) | async-done | bytes 4194320 | tf_op jit(solution)/shard_map/all_gather | solution.py:182
  268.8 1.6 copy-done.3
  270.4 1.6 copy-done.7
  272.0 7.3 shard_map.105
  279.4 1.5 pad_maximum_fusion
  280.8 129.5 %reduce-scatter.5.cloned.1.call-done = bf16[128,512]{1,0:T(8,128)(2,1)} async-done(((bf16[4096,512]{1,0:T(8,128)(2,1)}), bf16[128,512]{1,0:T(8,128)(2,1)}) %reduce-scatter.5.cloned.1.call-update) | async-done | bytes 131088 | tf_op jit(solution)/shard_map/reduce_scatter | solution.py:185
  410.3 139.0 %reduce-scatter.7.cloned.1.call-done = bf16[128,512]{1,0:T(8,128)(2,1)} async-done(((bf16[4096,512]{1,0:T(8,128)(2,1)}), bf16[128,512]{1,0:T(8,128)(2,1)}) %reduce-scatter.7.cloned.1.call-update) | async-done | bytes 131088 | tf_op jit(solution)/shard_map/reduce_scatter | solution.py:185
  549.4 139.3 %reduce-scatter.9.cloned.1.call-done = bf16[128,512]{1,0:T(8,128)(2,1)} async-done(((bf16[4096,512]{1,0:T(8,128)(2,1)}), bf16[128,512]{1,0:T(8,128)(2,1)}) %reduce-scatter.9.cloned.1.call-update) | async-done | bytes 131088 | tf_op jit(solution)/shard_map/reduce_scatter | solution.py:185
  688.7 139.3 %reduce-scatter.11.cloned.1.call-done = bf16[128,512]{1,0:T(8,128)(2,1)} async-done(((bf16[4096,512]{1,0:T(8,128)(2,1)}), bf16[128,512]{1,0:T(8,128)(2,1)}) %reduce-scatter.11.cloned.1.call-update) | async-done | bytes 131088 | tf_op jit(solution)/shard_map/reduce_scatter | solution.py:185
  831.5 13.4 %fusion.4 = f32[128,8192]{1,0:T(8,128)} fusion(bf16[128,1024]{0,1:T(8,128)(2,1)S(1)} %bitcast.25, bf16[8192,1024]{1,0:T(8,128)(2,1)} %param.11), kind=kOutput, calls=%fused_computation.10 | convolution fusion | flops 2147483648 | bytes 21233664 | tf_op jit(solution)/shard_map/rc,dc->rd/dot_general | solution.py:190
  846.5 13.9 %fusion = bf16[128,8192]{1,0:T(8,128)(2,1)} fusion(f32[128,8192]{1,0:T(8,128)} %fusion.4, bf16[128,1024]{0,1:T(8,128)(2,1)S(1)} %bitcast.23, bf16[8192,1024]{1,0:T(8,128)(2,1)} %param.12), kind=kOutput, calls=%fused_computation.1 | convolution fusion | flops 2149580800 | bytes 23330816 | tf_op jit(solution)/shard_map/rc,dc->rd/dot_general | solution.py:193
  (42 shorter events, 11.7 us)
Async XLA Ops:
  7.2 6.9 copy-start.8
  7.2 69.6 %all-gather.5.cloned.1.call-start = ((), (), s32[]{:S(2)}) async-start(), calls=%async_computation.4 | async-start | bytes 4325376 | tf_op jit(solution)/shard_map/all_gather | solution.py:182
  11.9 128.9 %all-gather.7.cloned.1.call-start = ((), (), s32[]{:S(2)}) async-start(), calls=%async_computation.5 | async-start | bytes 4325376 | tf_op jit(solution)/shard_map/all_gather | solution.py:182
  12.7 192.3 %all-gather.9.cloned.1.call-start = ((), (), s32[]{:S(2)}) async-start(), calls=%async_computation.6 | async-start | bytes 4325376 | tf_op jit(solution)/shard_map/all_gather | solution.py:182
  13.4 255.4 %all-gather.11.cloned.1.call-start = ((), (), s32[]{:S(2)}) async-start(), calls=%async_computation.7 | async-start | bytes 4325376 | tf_op jit(solution)/shard_map/all_gather | solution.py:182
  14.0 396.3 %reduce-scatter.5.cloned.1.call-start = ((), (), s32[]{:S(2)}) async-start(), calls=%async_computation.8 | async-start | bytes 4325376 | tf_op jit(solution)/shard_map/reduce_scatter | solution.py:185
  76.8 1.6 copy-start
  78.4 1.6 copy-start.4
  87.3 462.1 %reduce-scatter.7.cloned.1.call-start = ((), (), s32[]{:S(2)}) async-start(), calls=%async_computation.9 | async-start | bytes 4325376 | tf_op jit(solution)/shard_map/reduce_scatter | solution.py:185
  140.9 1.6 copy-start.1
  142.4 1.6 copy-start.5
  151.3 537.3 %reduce-scatter.9.cloned.1.call-start = ((), (), s32[]{:S(2)}) async-start(), calls=%async_computation.10 | async-start | bytes 4325376 | tf_op jit(solution)/shard_map/reduce_scatter | solution.py:185
  204.9 1.6 copy-start.2
  206.5 1.6 copy-start.6
  215.4 612.6 %reduce-scatter.11.cloned.1.call-start = ((), (), s32[]{:S(2)}) async-start(), calls=%async_computation.11 | async-start | bytes 4325376 | tf_op jit(solution)/shard_map/reduce_scatter | solution.py:185
  268.8 1.6 copy-start.3
  270.4 1.6 copy-start.7
Sparse Core Ops, SparseCore 0:
  12.0 64.7 all-gather.4
  80.2 60.5 all-gather.6
  144.3 60.5 all-gather.8
  208.2 60.5 all-gather.10
  271.0 139.3 reduce-scatter.4
  412.4 136.8 reduce-scatter.6
  551.6 136.9 reduce-scatter.8
  690.9 136.9 reduce-scatter.10
where the time goes:
time: 868 us; the launch traced here: 867 us
  waiting for transfers between devices  768 us (88%)
  Pallas kernels  29.1 us (3%)
  matrix products  27.4 us (3%)
  local copies, waits for them, and re-layouts  20.7 us (2%)
  between operations  17.2 us (2%)
    reduce_scatter x4, waiting for transfers between devices, shards(): sums.append(lax.psum_scatter(dkv, 'ctx', scatter_dimension=0, tiled=True))  547 us
    all_gather x4, waiting for transfers between devices, shards(): kv = lax.all_gather(part, 'ctx', tiled=True)  219 us
    pallas_call x4, Pallas kernels, attention(): pl.pallas_call(functools.partial(attention_kernel, tok_rows, keys // TILE...  29.1 us
  transfers between devices with their start and end apart: 8, of which 8 were waited for; matrix products, arithmetic and copies ran while one was open for 0% of the time, Pallas kernels for 3%

commit v1 on v0

--- a/solution.py
+++ b/solution.py
@@ -15,19 +15,45 @@
 DOC_MOST = 2048
 TILE = 256
 CHUNKS = 4
+PLANE = 8
+BACK = 2
 
 NEGATIVE = -1e30
 NT = (((1,), (1,)), ((), ()))
 
 
 def attention_kernel(
-    tok_rows, key_tiles, marks, pos_ref, first_ref, query_ref, cot_ref, kv_ref, dq_ref, dkv_ref,
-    query_rows, cot_rows, score_ref, weight_ref, dqt_ref,
+    tok_rows, key_tiles, marks, pos_ref, first_ref, query_ref, cot_ref, own_in, y_in, x_in, core_in,
+    dq_ref, own_out, y_out, x_out, core_out,
+    query_rows, cot_rows, score_ref, weight_ref, dqt_ref, kv_ref, dkv_ref,
 ):
     rows = GROUP * tok_rows
     soft_scale = 1.0 / math.sqrt(HD)
     exp2_scale = soft_scale * math.log2(math.e)
     low, full_low, full_high, high = marks[0], marks[1], marks[2], marks[3]
+    base, place = marks[4], marks[5]
+
+    blocks = [(own_in, own_out, plane, plane * PLANE + place) for plane in range(BACK + 1)]
+    for piece_in, piece_out, offsets in (
+        (y_in, y_out, (4,)), (x_in, x_out, (2, 6)), (core_in, core_out, (1, 5, 3, 7))
+    ):
+        for number, offset in enumerate(offsets):
+            source = place ^ offset
+            first_plane = jnp.where(source > place, 0, 1)
+            for plane in range(BACK):
+                blocks.append(
+                    (piece_in, piece_out, number * BACK + plane, (first_plane + plane) * PLANE + source)
+                )
+
+    def block_at(index):
+        return pl.ds(pl.multiple_of(index * tok_rows, tok_rows), tok_rows)
+
+    @pl.when(pl.program_id(0) == 0)
+    def _():
+        kv_ref[...] = jnp.zeros_like(kv_ref)
+
+    for piece_in, _, number, index in blocks:
+        kv_ref[block_at(index), :] = piece_in[number]
 
     for head in range(GROUP):
         query_rows[head * tok_rows:(head + 1) * tok_rows, :] = query_ref[:, head * HD:(head + 1) * HD]
@@ -47,7 +73,7 @@
             kv_ref[at(tile), :HD], query_rows[...], NT, preferred_element_type=jnp.float32
         )
         if masked:
-            key_pos = tile * TILE + lax.broadcasted_iota(jnp.int32, (TILE, rows), 0)
+            key_pos = (base + tile) * TILE + lax.broadcasted_iota(jnp.int32, (TILE, rows), 0)
             visible = (key_pos <= pos_ref[...]) & (key_pos >= first_ref[...])
             scores = jnp.where(visible, scores, NEGATIVE)
         score_ref[slot(tile), :] = scores
@@ -109,19 +135,25 @@
     lax.fori_loop(0, low, clear, 0)
     lax.fori_loop(high, key_tiles, clear, 0)
 
+    for _, piece_out, number, index in blocks:
+        piece_out[number] = dkv_ref[block_at(index), :]
+
     out_scale = inverse * soft_scale
     for head in range(GROUP):
         part = slice(head * tok_rows, (head + 1) * tok_rows)
         dq_ref[:, head * HD:(head + 1) * HD] = (dqt_ref[:, part] * out_scale[:, part]).T.astype(jnp.bfloat16)
 
 
-def attention(marks, pos, first, queries, grad_out, kv, tok_rows, first_head, heads_here):
+def attention(marks, pos, first, queries, grad_out, pieces, tok_rows, first_head, heads_here):
     rows = GROUP * tok_rows
-    keys = kv.shape[0]
+    keys = (BACK + 1) * PLANE * tok_rows
     slots = (DOC_MOST + tok_rows + 2 * TILE - 2) // TILE * TILE
     wide = GROUP * HD
-    flops = heads_here * 5 * 2 * rows * (DOC_MOST // 2) * HD
-    return pl.pallas_call(
+    flops = heads_here * 5 * 2 * rows * DOC_MOST * HD
+    piece_specs = [
+        pl.BlockSpec((piece.shape[0], tok_rows, 2 * HD), lambda h, marks: (0, 0, h)) for piece in pieces
+    ]
+    out = pl.pallas_call(
         functools.partial(attention_kernel, tok_rows, keys // TILE),
         grid_spec=pltpu.PrefetchScalarGridSpec(
             num_scalar_prefetch=1,
@@ -131,29 +163,131 @@
                 pl.BlockSpec((1, rows), lambda h, marks: (0, 0)),
                 pl.BlockSpec((tok_rows, wide), lambda h, marks: (0, first_head + h)),
                 pl.BlockSpec((tok_rows, wide), lambda h, marks: (0, first_head + h)),
-                pl.BlockSpec((keys, 2 * HD), lambda h, marks: (0, h)),
-            ],
-            out_specs=[
-                pl.BlockSpec((tok_rows, wide), lambda h, marks: (0, h)),
-                pl.BlockSpec((keys, 2 * HD), lambda h, marks: (0, h)),
-            ],
+            ] + piece_specs,
+            out_specs=[pl.BlockSpec((tok_rows, wide), lambda h, marks: (0, h))] + piece_specs,
             scratch_shapes=[
                 pltpu.VMEM((rows, HD), jnp.bfloat16),
                 pltpu.VMEM((rows, HD), jnp.bfloat16),
                 pltpu.VMEM((slots, rows), jnp.float32),
                 pltpu.VMEM((slots, rows), jnp.bfloat16),
                 pltpu.VMEM((HD, rows), jnp.float32),
+                pltpu.VMEM((keys, 2 * HD), jnp.bfloat16),
+                pltpu.VMEM((keys, 2 * HD), jnp.bfloat16),
             ],
         ),
-        out_shape=[
-            jax.ShapeDtypeStruct((tok_rows, heads_here * wide), jnp.bfloat16),
-            jax.ShapeDtypeStruct((keys, heads_here * 2 * HD), jnp.bfloat16),
-        ],
+        out_shape=[jax.ShapeDtypeStruct((tok_rows, heads_here * wide), jnp.bfloat16)]
+        + [jax.ShapeDtypeStruct(piece.shape, jnp.bfloat16) for piece in pieces],
         compiler_params=pltpu.CompilerParams(
-            dimension_semantics=("arbitrary",), vmem_limit_bytes=48 * 1024 * 1024
-        ),
-        cost_estimate=pl.CostEstimate(flops=flops * 4, bytes_accessed=heads_here * 4 * 1024 * 1024, transcendentals=0),
-    )(marks, pos, first, queries, grad_out, kv)
+            dimension_semantics=("arbitrary",), vmem_limit_bytes=40 * 1024 * 1024
+        ),
+        cost_estimate=pl.CostEstimate(
+            flops=flops * 2, bytes_accessed=heads_here * 4 * 1024 * 1024, transcendentals=0
+        ),
+    )(marks, pos, first, queries, grad_out, *pieces)
+    return out[0], out[1:]
+
+
+def swap(value, offset):
+    count = lax.axis_size("ctx")
+    return lax.ppermute(value, "ctx", [(source, source ^ offset) for source in range(count)])
+
+
+def move(value, steps):
+    count = lax.axis_size("ctx")
+    pairs = [(source, source + steps) for source in range(count) if 0 <= source + steps < count]
+    if not pairs:
+        return jnp.zeros_like(value)
+    return lax.ppermute(value, "ctx", pairs)
+
+
+def after(value, *earlier):
+    return lax.optimization_barrier((value, *earlier))[0]
+
+
+def seen_by(own, offset):
+    place = lax.axis_index("ctx") % PLANE
+    return jnp.where(place > (place ^ offset), own[:BACK], own[1:])
+
+
+def gather_far(part):
+    own = jnp.stack([move(part, PLANE * (BACK - plane)) for plane in range(BACK)] + [part])
+    return own, swap(seen_by(own, 4), 4)
+
+
+def gather_x(own, y_piece):
+    return swap(jnp.concatenate([seen_by(own, 2), y_piece]), 2)
+
+
+def gather_core(own, y_piece, x_piece):
+    return swap(jnp.concatenate([seen_by(own, 1), y_piece, x_piece]), 1)
+
+
+def widen(value):
+    return value.astype(jnp.float32)
+
+
+def placed(value, offset):
+    place = lax.axis_index("ctx") % PLANE
+    blank = jnp.zeros_like(value[:1])
+    early, late = jnp.concatenate([value, blank]), jnp.concatenate([blank, value])
+    return widen(jnp.where(place > (place ^ offset), early, late))
+
+
+def sum_core(pieces):
+    own, y_piece, x_piece, core_piece = pieces
+    got = swap(core_piece, 1)
+    x_sum = (widen(x_piece) + widen(got[2 * BACK:])).astype(jnp.bfloat16)
+    return own, y_piece, x_sum, got
+
+
+def sum_x(state):
+    own, y_piece, x_sum, from_core = state
+    got = swap(x_sum, 2)
+    y_sum = (widen(y_piece) + widen(from_core[BACK:2 * BACK]) + widen(got[BACK:])).astype(jnp.bfloat16)
+    return own, y_sum, from_core, got
+
+
+def sum_y(state):
+    own, y_sum, from_core, from_x = state
+    got = swap(y_sum, 4)
+    own_sum = widen(own) + placed(from_core[:BACK], 1) + placed(from_x[:BACK], 2) + placed(got, 4)
+    return own_sum.astype(jnp.bfloat16)
+
+
+def sum_far(own_sum):
+    total = widen(own_sum[BACK])
+    for plane in range(BACK):
+        total = total + widen(move(own_sum[plane], -PLANE * (BACK - plane)))
+    return total.astype(jnp.bfloat16)
+
+
+def input_kernel(key_ref, value_ref, key_weight_ref, value_weight_ref, out_ref):
+    total = lax.dot_general(key_ref[...], key_weight_ref[...], NT, preferred_element_type=jnp.float32)
+    total = total + lax.dot_general(
+        value_ref[...], value_weight_ref[...], NT, preferred_element_type=jnp.float32
+    )
+    out_ref[...] = total.astype(jnp.bfloat16)
+
+
+def input_gradient(grad_key, grad_value, key_weight, value_weight):
+    tok_rows, columns = grad_key.shape
+    width = key_weight.shape[0]
+    step = 512
+    held = pl.BlockSpec((tok_rows, columns), lambda d: (0, 0))
+    streamed = pl.BlockSpec((step, columns), lambda d: (d, 0))
+    return pl.pallas_call(
+        input_kernel,
+        grid=(width // step,),
+        in_specs=[held, held, streamed, streamed],
+        out_specs=pl.BlockSpec((tok_rows, step), lambda d: (0, d)),
+        out_shape=jax.ShapeDtypeStruct((tok_rows, width), jnp.bfloat16),
+        compiler_params=pltpu.CompilerParams(
+            dimension_semantics=("arbitrary",), vmem_limit_bytes=32 * 1024 * 1024
+        ),
+        cost_estimate=pl.CostEstimate(
+            flops=4 * tok_rows * columns * width, bytes_accessed=4 * width * columns, transcendentals=0
+        ),
+    )(grad_key, grad_value, key_weight, value_weight)
 
 
 def shards(queries, key_proj, value_proj, grad_out, key_weight, value_weight, doc_start):
@@ -167,7 +301,10 @@
     high = (begin + tok_rows + TILE - 1) // TILE
     full_low = jnp.minimum(full_low, high)
     full_high = jnp.maximum(full_high, full_low)
-    marks = jnp.stack([low, full_low, full_high, high]).astype(jnp.int32)
+    base = (my_index // PLANE - BACK) * PLANE * tok_rows // TILE
+    marks = jnp.stack(
+        [low - base, full_low - base, full_high - base, high - base, base, my_index % PLANE]
+    ).astype(jnp.int32)
     pos = jnp.tile(begin + jnp.arange(tok_rows, dtype=jnp.int32), GROUP)[None]
     first = jnp.tile(doc_start, GROUP)[None]
 
@@ -176,25 +313,43 @@
     pair = jnp.stack(
         [key_proj.reshape(tok_rows, heads_kv, HD), value_proj.reshape(tok_rows, heads_kv, HD)], axis=2
     ).reshape(tok_rows, heads_kv * 2 * HD)
-    grad_queries, sums = [], []
+    parts = [pair[:, chunk * per * 2 * HD:(chunk + 1) * per * 2 * HD] for chunk in range(chunks)]
+    far = [gather_far(part) for part in parts]
+    grad_queries, states, sums, done = [], [], [], []
+    stages = (sum_core, sum_x, sum_y)
     for chunk in range(chunks):
-        part = pair[:, chunk * per * 2 * HD:(chunk + 1) * per * 2 * HD]
-        kv = lax.all_gather(part, "ctx", tiled=True)
-        dq, dkv = attention(marks, pos, first, queries, grad_out, kv, tok_rows, chunk * per, per)
+        own, y_piece = far[chunk]
+        if chunk >= 3:
+            y_piece = after(y_piece, done[chunk - 3])
+        x_piece = gather_x(own, y_piece)
+        if chunk >= 2:
+            x_piece = after(x_piece, done[chunk - 2])
+        core_piece = gather_core(own, y_piece, x_piece)
+        held = []
+        for earlier in range(chunk - 1):
+            stage = chunk - 2 - earlier
+            if stage < len(stages):
+                states[earlier] = stages[stage](states[earlier])
+                held.append(states[earlier])
+        core_piece = after(core_piece, *jax.tree.leaves(held)) if held else core_piece
+        dq, partials = attention(
+            marks, pos, first, queries, grad_out, (own, y_piece, x_piece, core_piece), tok_rows, chunk * per, per
+        )
+        done.append(dq)
         grad_queries.append(dq)
-        sums.append(lax.psum_scatter(dkv, "ctx", scatter_dimension=0, tiled=True))
+        states.append(tuple(partials))
+    for chunk in range(chunks):
+        state = states[chunk]
+        for stage in stages[max(0, chunks - 2 - chunk + 0) if chunk < chunks - 1 else 0:]:
+            state = stage(state)
+        sums.append(sum_far(state))
     grad_query = jnp.concatenate(grad_queries, axis=1)
     both = jnp.concatenate(sums, axis=1).reshape(tok_rows, heads_kv, 2, HD)
     grad_key = both[:, :, 0].reshape(tok_rows, heads_kv * HD)
     grad_value = both[:, :, 1].reshape(tok_rows, heads_kv * HD)
-    partial_input = jnp.einsum(
-        "rc,dc->rd", grad_key, key_weight, preferred_element_type=jnp.float32
-    )
-    partial_input = partial_input + jnp.einsum(
-        "rc,dc->rd", grad_value, value_weight, preferred_element_type=jnp.float32
-    )
+    partial_input = input_gradient(grad_key, grad_value, key_weight, value_weight)
     grad_input = lax.psum_scatter(
-        partial_input.astype(jnp.bfloat16), "tp", scatter_dimension=1, tiled=True
+        partial_input, "tp", scatter_dimension=1, tiled=True
     )
     return (grad_query, grad_key, grad_value, grad_input)
 

time: 868 us -> 258 us (0.30)
  waiting for transfers between devices: 768 us -> 112 us
  starting transfers between devices: 0.5 us -> 81.4 us
  matrix products: 27.4 us -> 0 us
  between operations: 17.2 us -> 4.73 us
  Pallas kernels: 29.1 us -> 39.4 us
    reduce_scatter x4 -> x0, waiting for transfers between devices: 547 us -> none  [shards(): sums.append(lax.psum_scatter(dkv, 'ctx', scatter_dimension=0, tiled=True))]
    all_gather x4 -> x0, waiting for transfers between devices: 219 us -> none  [shards(): kv = lax.all_gather(part, 'ctx', tiled=True)]
    ppermute x0 -> x40, waiting for transfers between devices: none -> 112 us  [the longest x16 60.5 us: move(): return lax.ppermute(value, 'ctx', pairs)]
    ppermute x0 -> x40, starting transfers between devices: none -> 81.4 us  [the longest x16 46.3 us: move(): return lax.ppermute(value, 'ctx', pairs)]
    dot_general x2 -> x0, matrix products: 27.4 us -> none  [the longest x1 13.9 us: shards(): jnp.einsum('rc,dc->rd', grad_value, value_weight, preferred_element_type=...]
    pallas_call x0 -> x1, Pallas kernels: none -> 18.8 us  [input_gradient(): pl.pallas_call(input_kernel, grid=(width // step,), in_specs=[held, held,...]
    unnamed x22 -> x30, local copies, waits for them, and re-layouts: 15.5 us -> 6.02 us
  transfers between devices with their start and end apart: 8 -> 40, of which waited for: 8 -> 16; matrix products, arithmetic and copies ran while one was open for 0% -> 2% of each run, Pallas kernels for 3% -> 8%
where the time goes in v1:
time: 258 us; the launch traced here: 257 us
  waiting for transfers between devices  112 us (43%)
  starting transfers between devices  81.4 us (32%)
  Pallas kernels  39.4 us (15%)
  local copies, waits for them, and re-layouts  12.8 us (5%)
  other arithmetic  6.57 us (3%)
  between operations  4.73 us (2%)
    ppermute x16, waiting for transfers between devices, move(): return lax.ppermute(value, 'ctx', pairs)  60.5 us
    ppermute x24, waiting for transfers between devices, swap(): lax.ppermute(value, 'ctx', [(source, source ^ offset) for source in range...  51.9 us
    ppermute x16, starting transfers between devices, move(): return lax.ppermute(value, 'ctx', pairs)  46.3 us
    ppermute x24, starting transfers between devices, swap(): lax.ppermute(value, 'ctx', [(source, source ^ offset) for source in range...  35.1 us
    pallas_call x4, Pallas kernels, attention(): pl.pallas_call(functools.partial(attention_kernel, tok_rows, keys // TILE...  20.6 us
    pallas_call x1, Pallas kernels, input_gradient(): pl.pallas_call(input_kernel, grid=(width // step,), in_specs=[held, held,...  18.8 us
    unnamed x30, local copies, waits for them, and re-layouts  6.02 us
  transfers between devices with their start and end apart: 40, of which 16 were waited for; matrix products, arithmetic and copies ran while one was open for 2% of the time, Pallas kernels for 8%

profile of v1, /device:TPU:0, one launch (start us, length us, event | category | flops | bytes accessed | tf_op | source)
XLA Modules:
  0.0 257.3 jit_solution(295614700296642478)
XLA Ops:
  4.6 5.9 %collective-permute-start = (bf16[128,512]{1,0:T(8,128)(2,1)S(1)}, bf16[128,512]{1,0:T(8,128)(2,1)S(1)}, u32[]{:S(2)}, u32[]{:S(2)}) collective-permute-start(bf16[128,512]{1,0:T(8,128)(2,1)S(1)} %get-tuple-element.63), channel_id=1, source_target_pairs={{0,16},{1,17},{2,18},{3,19},{4,20},{5,21},{6,22},{7,23},{8,24},{9,... | collective-permute-start | bytes 393224 | tf_op jit(solution)/shard_map/ppermute | solution.py:200
  10.6 3.5 %collective-permute-start.1 = (bf16[128,512]{1,0:T(8,128)(2,1)S(1)}, bf16[128,512]{1,0:T(8,128)(2,1)S(1)}, u32[]{:S(2)}, u32[]{:S(2)}) collective-permute-start(bf16[128,512]{1,0:T(8,128)(2,1)S(1)} %get-tuple-element.63), channel_id=1, source_target_pairs={{0,8},{1,9},{2,10},{3,11},{4,12},{5,13},{6,14},{7,15},{8,16},{9,17... | collective-permute-start | bytes 393224 | tf_op jit(solution)/shard_map/ppermute | solution.py:200
  18.2 5.4 %collective-permute-done.2.y_in = bf16[2,128,512]{2,1,0:T(8,128)(2,1)S(1)} collective-permute-done((bf16[2,128,512]{2,1,0:T(8,128)(2,1)S(1)}, bf16[2,128,512]{2,1,0:T(8,128)(2,1)S(1)}, u32[]{:S(2)}, u32[]{:S(2)}) %collective-permute-start.2) | collective-permute-done | bytes 262176 | tf_op jit(solution)/shard_map/ppermute | solution.py:192
  25.2 9.0 %collective-permute-start.10 = (bf16[128,512]{1,0:T(8,128)(2,1)S(1)}, bf16[128,512]{1,0:T(8,128)(2,1)S(1)}, u32[]{:S(2)}, u32[]{:S(2)}) collective-permute-start(bf16[128,512]{1,0:T(8,128)(2,1)S(1)} %get-tuple-element.56), channel_id=1, source_target_pairs={{0,16},{1,17},{2,18},{3,19},{4,20},{5,21},{6,22},{7,23},{8,24},{9,... | collective-permute-start | bytes 393224 | tf_op jit(solution)/shard_map/ppermute | solution.py:200
  43.3 5.2 %collective-permute-start.16 = (bf16[128,512]{1,0:T(8,128)(2,1)S(1)}, bf16[128,512]{1,0:T(8,128)(2,1)S(1)}, u32[]{:S(2)}, u32[]{:S(2)}) collective-permute-start(bf16[128,512]{1,0:T(8,128)(2,1)S(1)} %get-tuple-element.61), channel_id=1, source_target_pairs={{0,16},{1,17},{2,18},{3,19},{4,20},{5,21},{6,22},{7,23},{8,24},{9,... | collective-permute-start | bytes 393224 | tf_op jit(solution)/shard_map/ppermute | solution.py:200
  48.5 7.2 %collective-permute-start.17 = (bf16[128,512]{1,0:T(8,128)(2,1)S(1)}, bf16[128,512]{1,0:T(8,128)(2,1)S(1)}, u32[]{:S(2)}, u32[]{:S(2)}) collective-permute-start(bf16[128,512]{1,0:T(8,128)(2,1)S(1)} %get-tuple-element.61), channel_id=1, source_target_pairs={{0,8},{1,9},{2,10},{3,11},{4,12},{5,13},{6,14},{7,15},{8,16},{9,17... | collective-permute-start | bytes 393224 | tf_op jit(solution)/shard_map/ppermute | solution.py:200
  58.3 5.4 %collective-permute-done.7.y_in = bf16[2,128,512]{2,1,0:T(8,128)(2,1)S(1)} collective-permute-done((bf16[2,128,512]{2,1,0:T(8,128)(2,1)S(1)}, bf16[2,128,512]{2,1,0:T(8,128)(2,1)S(1)}, u32[]{:S(2)}, u32[]{:S(2)}) %collective-permute-start.7) | collective-permute-done | bytes 262176 | tf_op jit(solution)/shard_map/ppermute | solution.py:192
  70.0 6.6 %collective-permute-done.8.x_in = bf16[4,128,512]{2,1,0:T(8,128)(2,1)S(1)} collective-permute-done((bf16[4,128,512]{2,1,0:T(8,128)(2,1)S(1)}, bf16[4,128,512]{2,1,0:T(8,128)(2,1)S(1)}, u32[]{:S(2)}, u32[]{:S(2)}) %collective-permute-start.8) | collective-permute-done | bytes 524320 | tf_op jit(solution)/shard_map/ppermute | solution.py:192
  76.9 5.2 %shard_map.102 = (bf16[128,2048]{1,0:T(8,128)(2,1)S(1)}, bf16[3,128,512]{2,1,0:T(8,128)(2,1)S(1)}, bf16[2,128,512]{2,1,0:T(8,128)(2,1)S(1)}, bf16[4,128,512]{2,1,0:T(8,128)(2,1)S(1)}, bf16[8,128,512]{2,1,0:T(8,128)(2,1)S(1)}) custom-call(s32[6]{0:T(128)S(1)} %stack.94.marks, s32[1,1024]{1,0:T(1,128)S(1)} %bitcast.68, s32[1,1024]{1,0:T(1,128)S(1)} %bitcast.72, ...), custom_call_target="tpu_custom_call" | custom-call | flops 10737418240 | bytes 8388608 | tf_op jit(solution)/shard_map/pallas_call | solution.py:156
  85.7 5.1 %shard_map.103 = (bf16[128,2048]{1,0:T(8,128)(2,1)S(1)}, bf16[3,128,512]{2,1,0:T(8,128)(2,1)S(1)}, bf16[2,128,512]{2,1,0:T(8,128)(2,1)S(1)}, bf16[4,128,512]{2,1,0:T(8,128)(2,1)S(1)}, bf16[8,128,512]{2,1,0:T(8,128)(2,1)S(1)}) custom-call(s32[6]{0:T(128)S(1)} %stack.94.marks, s32[1,1024]{1,0:T(1,128)S(1)} %bitcast.69, s32[1,1024]{1,0:T(1,128)S(1)} %bitcast.73, ...), custom_call_target="tpu_custom_call" | custom-call | flops 10737418240 | bytes 8388608 | tf_op jit(solution)/shard_map/pallas_call | solution.py:156
  91.1 7.9 %collective-permute-done.19.x_in = bf16[4,128,512]{2,1,0:T(8,128)(2,1)S(1)} collective-permute-done((bf16[4,128,512]{2,1,0:T(8,128)(2,1)S(1)}, bf16[4,128,512]{2,1,0:T(8,128)(2,1)S(1)}, u32[]{:S(2)}, u32[]{:S(2)}) %collective-permute-start.19) | collective-permute-done | bytes 524320 | tf_op jit(solution)/shard_map/ppermute | solution.py:192
  100.4 5.0 %shard_map.104 = (bf16[128,2048]{1,0:T(8,128)(2,1)S(1)}, bf16[3,128,512]{2,1,0:T(8,128)(2,1)S(1)}, bf16[2,128,512]{2,1,0:T(8,128)(2,1)S(1)}, bf16[4,128,512]{2,1,0:T(8,128)(2,1)S(1)}, bf16[8,128,512]{2,1,0:T(8,128)(2,1)S(1)}) custom-call(s32[6]{0:T(128)S(1)} %stack.94.marks, s32[1,1024]{1,0:T(1,128)S(1)} %bitcast.70, s32[1,1024]{1,0:T(1,128)S(1)} %bitcast.74, ...), custom_call_target="tpu_custom_call" | custom-call | flops 10737418240 | bytes 8388608 | tf_op jit(solution)/shard_map/pallas_call | solution.py:156
  109.2 4.9 %collective-permute-done.21 = bf16[4,128,512]{2,1,0:T(8,128)(2,1)S(1)} collective-permute-done((bf16[4,128,512]{2,1,0:T(8,128)(2,1)S(1)}, bf16[4,128,512]{2,1,0:T(8,128)(2,1)S(1)}, u32[]{:S(2)}, u32[]{:S(2)}) %collective-permute-start.21) | collective-permute-done | bytes 524320 | tf_op jit(solution)/shard_map/ppermute | solution.py:192
  114.2 8.1 %collective-permute-start.23 = (bf16[2,128,512]{2,1,0:T(8,128)(2,1)S(1)}, bf16[2,128,512]{2,1,0:T(8,128)(2,1)S(1)}, u32[]{:S(2)}, u32[]{:S(2)}) collective-permute-start(bf16[2,128,512]{2,1,0:T(8,128)(2,1)S(1)} %add_convert_fusion.11), channel_id=1, source_target_pairs={{0,4},{1,5},{2,6},{3,7},{4,0},{5,1},{6,2},{7,3},{8,12},{9,13},{10,... | collective-permute-start | bytes 786440 | tf_op jit(solution)/shard_map/ppermute | solution.py:192
  122.3 5.3 %shard_map.105 = (bf16[128,2048]{1,0:T(8,128)(2,1)S(1)}, bf16[3,128,512]{2,1,0:T(8,128)(2,1)S(1)}, bf16[2,128,512]{2,1,0:T(8,128)(2,1)S(1)}, bf16[4,128,512]{2,1,0:T(8,128)(2,1)S(1)}, bf16[8,128,512]{2,1,0:T(8,128)(2,1)S(1)}) custom-call(s32[6]{0:T(128)S(1)} %stack.94.marks, s32[1,1024]{1,0:T(1,128)S(1)} %bitcast.71, s32[1,1024]{1,0:T(1,128)S(1)} %bitcast.75, ...), custom_call_target="tpu_custom_call" | custom-call | flops 10737418240 | bytes 8388608 | tf_op jit(solution)/shard_map/pallas_call | solution.py:156
  127.8 6.9 %collective-permute-start.27 = (bf16[2,128,512]{2,1,0:T(8,128)(2,1)S(1)}, bf16[2,128,512]{2,1,0:T(8,128)(2,1)S(1)}, u32[]{:S(2)}, u32[]{:S(2)}) collective-permute-start(bf16[2,128,512]{2,1,0:T(8,128)(2,1)S(1)} %add_convert_fusion.10), channel_id=1, source_target_pairs={{0,4},{1,5},{2,6},{3,7},{4,0},{5,1},{6,2},{7,3},{8,12},{9,13},{10,... | collective-permute-start | bytes 786440 | tf_op jit(solution)/shard_map/ppermute | solution.py:192
  138.1 10.7 %collective-permute-done.31 = bf16[4,128,512]{2,1,0:T(8,128)(2,1)S(1)} collective-permute-done((bf16[4,128,512]{2,1,0:T(8,128)(2,1)S(1)}, bf16[4,128,512]{2,1,0:T(8,128)(2,1)S(1)}, u32[]{:S(2)}, u32[]{:S(2)}) %collective-permute-start.31) | collective-permute-done | bytes 524320 | tf_op jit(solution)/shard_map/ppermute | solution.py:192
  151.3 5.2 %collective-permute-done.32 = bf16[2,128,512]{2,1,0:T(8,128)(2,1)S(1)} collective-permute-done((bf16[2,128,512]{2,1,0:T(8,128)(2,1)S(1)}, bf16[2,128,512]{2,1,0:T(8,128)(2,1)S(1)}, u32[]{:S(2)}, u32[]{:S(2)}) %collective-permute-start.32) | collective-permute-done | bytes 262176 | tf_op jit(solution)/shard_map/ppermute | solution.py:192
  165.8 32.4 %collective-permute-done.25 = bf16[128,512]{1,0:T(8,128)(2,1)S(1)} collective-permute-done((bf16[128,512]{1,0:T(8,128)(2,1)S(1)}, bf16[128,512]{1,0:T(8,128)(2,1)S(1)}, u32[]{:S(2)}, u32[]{:S(2)}) %collective-permute-start.25) | collective-permute-done | bytes 131104 | tf_op jit(solution)/shard_map/ppermute | solution.py:200
  198.3 9.7 %collective-permute-done.33 = bf16[128,512]{1,0:T(8,128)(2,1)S(1)} collective-permute-done((bf16[128,512]{1,0:T(8,128)(2,1)S(1)}, bf16[128,512]{1,0:T(8,128)(2,1)S(1)}, u32[]{:S(2)}, u32[]{:S(2)}) %collective-permute-start.33) | collective-permute-done | bytes 131104 | tf_op jit(solution)/shard_map/ppermute | solution.py:200
  214.2 7.9 %collective-permute-done.28 = bf16[128,512]{1,0:T(8,128)(2,1)S(1)} collective-permute-done((bf16[128,512]{1,0:T(8,128)(2,1)S(1)}, bf16[128,512]{1,0:T(8,128)(2,1)S(1)}, u32[]{:S(2)}, u32[]{:S(2)}) %collective-permute-start.28) | collective-permute-done | bytes 131104 | tf_op jit(solution)/shard_map/ppermute | solution.py:200
  222.2 7.0 %collective-permute-done.38 = bf16[128,512]{1,0:T(8,128)(2,1)S(1)} collective-permute-done((bf16[128,512]{1,0:T(8,128)(2,1)S(1)}, bf16[128,512]{1,0:T(8,128)(2,1)S(1)}, u32[]{:S(2)}, u32[]{:S(2)}) %collective-permute-start.38) | collective-permute-done | bytes 131104 | tf_op jit(solution)/shard_map/ppermute | solution.py:200
  232.5 5.9 %copy-done = bf16[8192,1024]{1,0:T(8,128)(2,1)S(1)} copy-done((bf16[8192,1024]{1,0:T(8,128)(2,1)S(1)}, bf16[8192,1024]{1,0:T(8,128)(2,1)}, u32[]{:S(2)}) %copy-start) | copy-done | bytes 16777240
  238.4 18.8 %shard_map.106 = bf16[128,8192]{1,0:T(8,128)(2,1)} custom-call(bf16[128,1024]{1,0:T(8,128)(2,1)S(1)} %get-tuple-element.91.key_ref, bf16[128,1024]{1,0:T(8,128)(2,1)S(1)} %get-tuple-element.90.value_ref, bf16[8192,1024]{1,0:T(8,128)(2,1)S(1)} %copy-done, bf16[8192,1024]{1,0:T(8,128)(2,1)} %value_weight_ref.1), custom_call_target="tpu_custom_call" | custom-call | flops 4294967296 | bytes 33554432 | tf_op jit(solution)/shard_map/pallas_call | solution.py:278
  (152 shorter events, 58.3 us)
Async XLA Ops:
  23.6 32.2 %collective-permute-start.3 = (bf16[4,128,512]{2,1,0:T(8,128)(2,1)S(1)}, bf16[4,128,512]{2,1,0:T(8,128)(2,1)S(1)}, u32[]{:S(2)}, u32[]{:S(2)}) collective-permute-start(bf16[4,128,512]{2,1,0:T(8,128)(2,1)S(1)} %pad_maximum_fusion.6), channel_id=1, source_target_pairs={{0,2},{1,3},{2,0},{3,1},{4,6},{5,7},{6,4},{7,5},{8,10},{9,11},{10,... | collective-permute-start | bytes 1572872 | tf_op jit(solution)/shard_map/ppermute | solution.py:192
  25.2 32.3 %collective-permute-start.10 = (bf16[128,512]{1,0:T(8,128)(2,1)S(1)}, bf16[128,512]{1,0:T(8,128)(2,1)S(1)}, u32[]{:S(2)}, u32[]{:S(2)}) collective-permute-start(bf16[128,512]{1,0:T(8,128)(2,1)S(1)} %get-tuple-element.56), channel_id=1, source_target_pairs={{0,16},{1,17},{2,18},{3,19},{4,20},{5,21},{6,22},{7,23},{8,24},{9,... | collective-permute-start | bytes 393224 | tf_op jit(solution)/shard_map/ppermute | solution.py:200
  34.2 23.4 %collective-permute-start.11 = (bf16[128,512]{1,0:T(8,128)(2,1)S(1)}, bf16[128,512]{1,0:T(8,128)(2,1)S(1)}, u32[]{:S(2)}, u32[]{:S(2)}) collective-permute-start(bf16[128,512]{1,0:T(8,128)(2,1)S(1)} %get-tuple-element.56), channel_id=1, source_target_pairs={{0,8},{1,9},{2,10},{3,11},{4,12},{5,13},{6,14},{7,15},{8,16},{9,17... | collective-permute-start | bytes 393224 | tf_op jit(solution)/shard_map/ppermute | solution.py:200
  43.3 21.1 %collective-permute-start.16 = (bf16[128,512]{1,0:T(8,128)(2,1)S(1)}, bf16[128,512]{1,0:T(8,128)(2,1)S(1)}, u32[]{:S(2)}, u32[]{:S(2)}) collective-permute-start(bf16[128,512]{1,0:T(8,128)(2,1)S(1)} %get-tuple-element.61), channel_id=1, source_target_pairs={{0,16},{1,17},{2,18},{3,19},{4,20},{5,21},{6,22},{7,23},{8,24},{9,... | collective-permute-start | bytes 393224 | tf_op jit(solution)/shard_map/ppermute | solution.py:200
  48.5 15.9 %collective-permute-start.17 = (bf16[128,512]{1,0:T(8,128)(2,1)S(1)}, bf16[128,512]{1,0:T(8,128)(2,1)S(1)}, u32[]{:S(2)}, u32[]{:S(2)}) collective-permute-start(bf16[128,512]{1,0:T(8,128)(2,1)S(1)} %get-tuple-element.61), channel_id=1, source_target_pairs={{0,8},{1,9},{2,10},{3,11},{4,12},{5,13},{6,14},{7,15},{8,16},{9,17... | collective-permute-start | bytes 393224 | tf_op jit(solution)/shard_map/ppermute | solution.py:200
  57.5 19.3 %collective-permute-start.4 = (bf16[8,128,512]{2,1,0:T(8,128)(2,1)S(1)}, bf16[8,128,512]{2,1,0:T(8,128)(2,1)S(1)}, u32[]{:S(2)}, u32[]{:S(2)}) collective-permute-start(bf16[8,128,512]{2,1,0:T(8,128)(2,1)S(1)} %pad_maximum_fusion.1), channel_id=1, source_target_pairs={{0,1},{1,0},{2,3},{3,2},{4,5},{5,4},{6,7},{7,6},{8,9},{9,8},{10,11... | collective-permute-start | bytes 3145736 | tf_op jit(solution)/shard_map/ppermute | solution.py:192
  64.5 20.4 %collective-permute-start.18 = (bf16[2,128,512]{2,1,0:T(8,128)(2,1)S(1)}, bf16[2,128,512]{2,1,0:T(8,128)(2,1)S(1)}, u32[]{:S(2)}, u32[]{:S(2)}) collective-permute-start(bf16[2,128,512]{2,1,0:T(8,128)(2,1)S(1)} %get-tuple-element.77), channel_id=1, source_target_pairs={{0,4},{1,5},{2,6},{3,7},{4,0},{5,1},{6,2},{7,3},{8,12},{9,13},{10,... | collective-permute-start | bytes 786440 | tf_op jit(solution)/shard_map/ppermute | solution.py:192
  69.4 14.9 %collective-permute-start.13 = (bf16[4,128,512]{2,1,0:T(8,128)(2,1)S(1)}, bf16[4,128,512]{2,1,0:T(8,128)(2,1)S(1)}, u32[]{:S(2)}, u32[]{:S(2)}) collective-permute-start(bf16[4,128,512]{2,1,0:T(8,128)(2,1)S(1)} %pad_maximum_fusion.8), channel_id=1, source_target_pairs={{0,2},{1,3},{2,0},{3,1},{4,6},{5,7},{6,4},{7,5},{8,10},{9,11},{10,... | collective-permute-start | bytes 1572872 | tf_op jit(solution)/shard_map/ppermute | solution.py:192
  84.4 16.1 %collective-permute-start.14 = (bf16[8,128,512]{2,1,0:T(8,128)(2,1)S(1)}, bf16[8,128,512]{2,1,0:T(8,128)(2,1)S(1)}, u32[]{:S(2)}, u32[]{:S(2)}) collective-permute-start(bf16[8,128,512]{2,1,0:T(8,128)(2,1)S(1)} %pad_maximum_fusion.3), channel_id=1, source_target_pairs={{0,1},{1,0},{2,3},{3,2},{4,5},{5,4},{6,7},{7,6},{8,9},{9,8},{10,11... | collective-permute-start | bytes 3145736 | tf_op jit(solution)/shard_map/ppermute | solution.py:192
  84.5 14.7 %collective-permute-start.15 = (bf16[8,128,512]{2,1,0:T(8,128)(2,1)S(1)}, bf16[8,128,512]{2,1,0:T(8,128)(2,1)S(1)}, u32[]{:S(2)}, u32[]{:S(2)}) collective-permute-start(bf16[8,128,512]{2,1,0:T(8,128)(2,1)S(1)} %get-tuple-element.35), channel_id=1, source_target_pairs={{0,1},{1,0},{2,3},{3,2},{4,5},{5,4},{6,7},{7,6},{8,9},{9,8},{10,11... | collective-permute-start | bytes 3145736 | tf_op jit(solution)/shard_map/ppermute | solution.py:192
  90.8 15.0 %collective-permute-start.22 = (bf16[8,128,512]{2,1,0:T(8,128)(2,1)S(1)}, bf16[8,128,512]{2,1,0:T(8,128)(2,1)S(1)}, u32[]{:S(2)}, u32[]{:S(2)}) collective-permute-start(bf16[8,128,512]{2,1,0:T(8,128)(2,1)S(1)} %get-tuple-element.43), channel_id=1, source_target_pairs={{0,1},{1,0},{2,3},{3,2},{4,5},{5,4},{6,7},{7,6},{8,9},{9,8},{10,11... | collective-permute-start | bytes 3145736 | tf_op jit(solution)/shard_map/ppermute | solution.py:192
  99.1 23.2 %collective-permute-start.20 = (bf16[8,128,512]{2,1,0:T(8,128)(2,1)S(1)}, bf16[8,128,512]{2,1,0:T(8,128)(2,1)S(1)}, u32[]{:S(2)}, u32[]{:S(2)}) collective-permute-start(bf16[8,128,512]{2,1,0:T(8,128)(2,1)S(1)} %pad_maximum_fusion.4), channel_id=1, source_target_pairs={{0,1},{1,0},{2,3},{3,2},{4,5},{5,4},{6,7},{7,6},{8,9},{9,8},{10,11... | collective-permute-start | bytes 3145736 | tf_op jit(solution)/shard_map/ppermute | solution.py:192
  99.3 14.8 %collective-permute-start.21 = (bf16[4,128,512]{2,1,0:T(8,128)(2,1)S(1)}, bf16[4,128,512]{2,1,0:T(8,128)(2,1)S(1)}, u32[]{:S(2)}, u32[]{:S(2)}) collective-permute-start(bf16[4,128,512]{2,1,0:T(8,128)(2,1)S(1)} %add_convert_fusion.3), channel_id=1, source_target_pairs={{0,2},{1,3},{2,0},{3,1},{4,6},{5,7},{6,4},{7,5},{8,10},{9,11},{10,... | collective-permute-start | bytes 1572872 | tf_op jit(solution)/shard_map/ppermute | solution.py:192
  105.5 29.2 %collective-permute-start.30 = (bf16[8,128,512]{2,1,0:T(8,128)(2,1)S(1)}, bf16[8,128,512]{2,1,0:T(8,128)(2,1)S(1)}, u32[]{:S(2)}, u32[]{:S(2)}) collective-permute-start(bf16[8,128,512]{2,1,0:T(8,128)(2,1)S(1)} %get-tuple-element.47), channel_id=1, source_target_pairs={{0,1},{1,0},{2,3},{3,2},{4,5},{5,4},{6,7},{7,6},{8,9},{9,8},{10,11... | collective-permute-start | bytes 3145736 | tf_op jit(solution)/shard_map/ppermute | solution.py:192
  105.9 21.7 %collective-permute-start.26 = (bf16[4,128,512]{2,1,0:T(8,128)(2,1)S(1)}, bf16[4,128,512]{2,1,0:T(8,128)(2,1)S(1)}, u32[]{:S(2)}, u32[]{:S(2)}) collective-permute-start(bf16[4,128,512]{2,1,0:T(8,128)(2,1)S(1)} %add_convert_fusion.2), channel_id=1, source_target_pairs={{0,2},{1,3},{2,0},{3,1},{4,6},{5,7},{6,4},{7,5},{8,10},{9,11},{10,... | collective-permute-start | bytes 1572872 | tf_op jit(solution)/shard_map/ppermute | solution.py:192
  114.2 37.1 %collective-permute-start.23 = (bf16[2,128,512]{2,1,0:T(8,128)(2,1)S(1)}, bf16[2,128,512]{2,1,0:T(8,128)(2,1)S(1)}, u32[]{:S(2)}, u32[]{:S(2)}) collective-permute-start(bf16[2,128,512]{2,1,0:T(8,128)(2,1)S(1)} %add_convert_fusion.11), channel_id=1, source_target_pairs={{0,4},{1,5},{2,6},{3,7},{4,0},{5,1},{6,2},{7,3},{8,12},{9,13},{10,... | collective-permute-start | bytes 786440 | tf_op jit(solution)/shard_map/ppermute | solution.py:192
  127.6 21.7 %collective-permute-start.35 = (bf16[8,128,512]{2,1,0:T(8,128)(2,1)S(1)}, bf16[8,128,512]{2,1,0:T(8,128)(2,1)S(1)}, u32[]{:S(2)}, u32[]{:S(2)}) collective-permute-start(bf16[8,128,512]{2,1,0:T(8,128)(2,1)S(1)} %get-tuple-element.51), channel_id=1, source_target_pairs={{0,1},{1,0},{2,3},{3,2},{4,5},{5,4},{6,7},{7,6},{8,9},{9,8},{10,11... | collective-permute-start | bytes 3145736 | tf_op jit(solution)/shard_map/ppermute | solution.py:192
  127.8 80.3 %collective-permute-start.27 = (bf16[2,128,512]{2,1,0:T(8,128)(2,1)S(1)}, bf16[2,128,512]{2,1,0:T(8,128)(2,1)S(1)}, u32[]{:S(2)}, u32[]{:S(2)}) collective-permute-start(bf16[2,128,512]{2,1,0:T(8,128)(2,1)S(1)} %add_convert_fusion.10), channel_id=1, source_target_pairs={{0,4},{1,5},{2,6},{3,7},{4,0},{5,1},{6,2},{7,3},{8,12},{9,13},{10,... | collective-permute-start | bytes 786440 | tf_op jit(solution)/shard_map/ppermute | solution.py:192
  158.8 39.4 %collective-permute-start.25 = (bf16[128,512]{1,0:T(8,128)(2,1)S(1)}, bf16[128,512]{1,0:T(8,128)(2,1)S(1)}, u32[]{:S(2)}, u32[]{:S(2)}) collective-permute-start(bf16[128,512]{1,0:T(8,128)(2,1)S(1)} %get-tuple-element.65), channel_id=1, source_target_pairs={{8,0},{9,1},{10,2},{11,3},{12,4},{13,5},{14,6},{15,7},{16,8},{17,9... | collective-permute-start | bytes 393224 | tf_op jit(solution)/shard_map/ppermute | solution.py:200
  160.1 47.9 %collective-permute-start.33 = (bf16[128,512]{1,0:T(8,128)(2,1)S(1)}, bf16[128,512]{1,0:T(8,128)(2,1)S(1)}, u32[]{:S(2)}, u32[]{:S(2)}) collective-permute-start(bf16[128,512]{1,0:T(8,128)(2,1)S(1)} %get-tuple-element.68), channel_id=1, source_target_pairs={{16,0},{17,1},{18,2},{19,3},{20,4},{21,5},{22,6},{23,7},{24,8},{25... | collective-permute-start | bytes 393224 | tf_op jit(solution)/shard_map/ppermute | solution.py:200
  162.7 45.3 %collective-permute-start.34 = (bf16[128,512]{1,0:T(8,128)(2,1)S(1)}, bf16[128,512]{1,0:T(8,128)(2,1)S(1)}, u32[]{:S(2)}, u32[]{:S(2)}) collective-permute-start(bf16[128,512]{1,0:T(8,128)(2,1)S(1)} %get-tuple-element.69), channel_id=1, source_target_pairs={{8,0},{9,1},{10,2},{11,3},{12,4},{13,5},{14,6},{15,7},{16,8},{17,9... | collective-permute-start | bytes 393224 | tf_op jit(solution)/shard_map/ppermute | solution.py:200
  165.2 42.8 %collective-permute-start.37 = (bf16[2,128,512]{2,1,0:T(8,128)(2,1)S(1)}, bf16[2,128,512]{2,1,0:T(8,128)(2,1)S(1)}, u32[]{:S(2)}, u32[]{:S(2)}) collective-permute-start(bf16[2,128,512]{2,1,0:T(8,128)(2,1)S(1)} %add_convert_fusion.8), channel_id=1, source_target_pairs={{0,4},{1,5},{2,6},{3,7},{4,0},{5,1},{6,2},{7,3},{8,12},{9,13},{10,... | collective-permute-start | bytes 786440 | tf_op jit(solution)/shard_map/ppermute | solution.py:192
  211.6 17.5 %collective-permute-start.38 = (bf16[128,512]{1,0:T(8,128)(2,1)S(1)}, bf16[128,512]{1,0:T(8,128)(2,1)S(1)}, u32[]{:S(2)}, u32[]{:S(2)}) collective-permute-start(bf16[128,512]{1,0:T(8,128)(2,1)S(1)} %get-tuple-element.70), channel_id=1, source_target_pairs={{16,0},{17,1},{18,2},{19,3},{20,4},{21,5},{22,6},{23,7},{24,8},{25... | collective-permute-start | bytes 393224 | tf_op jit(solution)/shard_map/ppermute | solution.py:200
  212.9 16.2 %collective-permute-start.39 = (bf16[128,512]{1,0:T(8,128)(2,1)S(1)}, bf16[128,512]{1,0:T(8,128)(2,1)S(1)}, u32[]{:S(2)}, u32[]{:S(2)}) collective-permute-start(bf16[128,512]{1,0:T(8,128)(2,1)S(1)} %get-tuple-element.71), channel_id=1, source_target_pairs={{8,0},{9,1},{10,2},{11,3},{12,4},{13,5},{14,6},{15,7},{16,8},{17,9... | collective-permute-start | bytes 393224 | tf_op jit(solution)/shard_map/ppermute | solution.py:200
  (35 other events, 670.3 us)

commit v2 on v1

--- a/solution.py
+++ b/solution.py
@@ -314,14 +314,18 @@
         [key_proj.reshape(tok_rows, heads_kv, HD), value_proj.reshape(tok_rows, heads_kv, HD)], axis=2
     ).reshape(tok_rows, heads_kv * 2 * HD)
     parts = [pair[:, chunk * per * 2 * HD:(chunk + 1) * per * 2 * HD] for chunk in range(chunks)]
-    far = [gather_far(part) for part in parts]
+    far = [gather_far(parts[0])]
+    first_x = gather_x(*far[0])
+    far += [
+        gather_far(after(part, far[0][1] if chunk == 0 else first_x)) for chunk, part in enumerate(parts[1:])
+    ]
     grad_queries, states, sums, done = [], [], [], []
     stages = (sum_core, sum_x, sum_y)
     for chunk in range(chunks):
         own, y_piece = far[chunk]
         if chunk >= 3:
             y_piece = after(y_piece, done[chunk - 3])
-        x_piece = gather_x(own, y_piece)
+        x_piece = gather_x(own, y_piece) if chunk else first_x
         if chunk >= 2:
             x_piece = after(x_piece, done[chunk - 2])
         core_piece = gather_core(own, y_piece, x_piece)

time: 258 us -> 241 us (0.934)
  waiting for transfers between devices: 112 us -> 95.5 us
    ppermute x24, waiting for transfers between devices: 51.9 us -> 36.8 us  [swap(): lax.ppermute(value, 'ctx', [(source, source ^ offset) for source in range...]
    ppermute x16, starting transfers between devices: 46.3 us -> 42.2 us  [move(): return lax.ppermute(value, 'ctx', pairs)]
    ppermute x24, starting transfers between devices: 35.1 us -> 38.9 us  [swap(): lax.ppermute(value, 'ctx', [(source, source ^ offset) for source in range...]
    unnamed x30 -> x26, local copies, waits for them, and re-layouts: 6.02 us -> 6.01 us
  transfers between devices with their start and end apart: 40 -> 40, of which waited for: 16 -> 16; matrix products, arithmetic and copies ran while one was open for 2% -> 2% of each run, Pallas kernels for 8% -> 9%
where the time goes in v2:
time: 241 us; the launch traced here: 240 us
  waiting for transfers between devices  95.5 us (40%)
  starting transfers between devices  81.1 us (34%)
  Pallas kernels  39.4 us (16%)
  local copies, waits for them, and re-layouts  12.8 us (5%)
  other arithmetic  6.57 us (3%)
  between operations  4.73 us (2%)
    ppermute x16, waiting for transfers between devices, move(): return lax.ppermute(value, 'ctx', pairs)  58.7 us
    ppermute x16, starting transfers between devices, move(): return lax.ppermute(value, 'ctx', pairs)  42.2 us
    ppermute x24, starting transfers between devices, swap(): lax.ppermute(value, 'ctx', [(source, source ^ offset) for source in range...  38.9 us
    ppermute x24, waiting for transfers between devices, swap(): lax.ppermute(value, 'ctx', [(source, source ^ offset) for source in range...  36.8 us
    pallas_call x4, Pallas kernels, attention(): pl.pallas_call(functools.partial(attention_kernel, tok_rows, keys // TILE...  20.6 us
    pallas_call x1, Pallas kernels, input_gradient(): pl.pallas_call(input_kernel, grid=(width // step,), in_specs=[held, held,...  18.8 us
    unnamed x26, local copies, waits for them, and re-layouts  6.01 us
  transfers between devices with their start and end apart: 40, of which 16 were waited for; matrix products, arithmetic and copies ran while one was open for 2% of the time, Pallas kernels for 9%

profile of v2, /device:TPU:0, one launch (start us, length us, event | category | flops | bytes accessed | tf_op | source)
XLA Modules:
  0.0 240.1 jit_solution(17797751038364028871)
XLA Ops:
  4.6 5.9 %collective-permute-start = (bf16[128,512]{1,0:T(8,128)(2,1)S(1)}, bf16[128,512]{1,0:T(8,128)(2,1)S(1)}, u32[]{:S(2)}, u32[]{:S(2)}) collective-permute-start(bf16[128,512]{1,0:T(8,128)(2,1)S(1)} %get-tuple-element.66), channel_id=1, source_target_pairs={{0,16},{1,17},{2,18},{3,19},{4,20},{5,21},{6,22},{7,23},{8,24},{9,... | collective-permute-start | bytes 393224 | tf_op jit(solution)/shard_map/ppermute | solution.py:200
  10.5 3.5 %collective-permute-start.1 = (bf16[128,512]{1,0:T(8,128)(2,1)S(1)}, bf16[128,512]{1,0:T(8,128)(2,1)S(1)}, u32[]{:S(2)}, u32[]{:S(2)}) collective-permute-start(bf16[128,512]{1,0:T(8,128)(2,1)S(1)} %get-tuple-element.66), channel_id=1, source_target_pairs={{0,8},{1,9},{2,10},{3,11},{4,12},{5,13},{6,14},{7,15},{8,16},{9,17... | collective-permute-start | bytes 393224 | tf_op jit(solution)/shard_map/ppermute | solution.py:200
  18.2 5.4 %collective-permute-done.2.y_in = bf16[2,128,512]{2,1,0:T(8,128)(2,1)S(1)} collective-permute-done((bf16[2,128,512]{2,1,0:T(8,128)(2,1)S(1)}, bf16[2,128,512]{2,1,0:T(8,128)(2,1)S(1)}, u32[]{:S(2)}, u32[]{:S(2)}) %collective-permute-start.2) | collective-permute-done | bytes 262176 | tf_op jit(solution)/shard_map/ppermute | solution.py:192
  25.2 9.0 %collective-permute-start.5 = (bf16[128,512]{1,0:T(8,128)(2,1)S(1)}, bf16[128,512]{1,0:T(8,128)(2,1)S(1)}, u32[]{:S(2)}, u32[]{:S(2)}) collective-permute-start(bf16[128,512]{1,0:T(8,128)(2,1)S(1)} %get-tuple-element.33), channel_id=1, source_target_pairs={{0,16},{1,17},{2,18},{3,19},{4,20},{5,21},{6,22},{7,23},{8,24},{9,... | collective-permute-start | bytes 393224 | tf_op jit(solution)/shard_map/ppermute | solution.py:200
  41.4 5.3 %collective-permute-start.10 = (bf16[128,512]{1,0:T(8,128)(2,1)S(1)}, bf16[128,512]{1,0:T(8,128)(2,1)S(1)}, u32[]{:S(2)}, u32[]{:S(2)}) collective-permute-start(bf16[128,512]{1,0:T(8,128)(2,1)S(1)} %get-tuple-element.35), channel_id=1, source_target_pairs={{0,16},{1,17},{2,18},{3,19},{4,20},{5,21},{6,22},{7,23},{8,24},{9,... | collective-permute-start | bytes 393224 | tf_op jit(solution)/shard_map/ppermute | solution.py:200
  48.9 4.3 %collective-permute-start.16 = (bf16[128,512]{1,0:T(8,128)(2,1)S(1)}, bf16[128,512]{1,0:T(8,128)(2,1)S(1)}, u32[]{:S(2)}, u32[]{:S(2)}) collective-permute-start(bf16[128,512]{1,0:T(8,128)(2,1)S(1)} %get-tuple-element.43), channel_id=1, source_target_pairs={{0,16},{1,17},{2,18},{3,19},{4,20},{5,21},{6,22},{7,23},{8,24},{9,... | collective-permute-start | bytes 393224 | tf_op jit(solution)/shard_map/ppermute | solution.py:200
  65.6 5.2 %shard_map.102 = (bf16[128,2048]{1,0:T(8,128)(2,1)S(1)}, bf16[3,128,512]{2,1,0:T(8,128)(2,1)S(1)}, bf16[2,128,512]{2,1,0:T(8,128)(2,1)S(1)}, bf16[4,128,512]{2,1,0:T(8,128)(2,1)S(1)}, bf16[8,128,512]{2,1,0:T(8,128)(2,1)S(1)}) custom-call(s32[6]{0:T(128)S(1)} %stack.94.marks, s32[1,1024]{1,0:T(1,128)S(1)} %bitcast.65, s32[1,1024]{1,0:T(1,128)S(1)} %bitcast.69, ...), custom_call_target="tpu_custom_call" | custom-call | flops 10737418240 | bytes 8388608 | tf_op jit(solution)/shard_map/pallas_call | solution.py:156
  75.3 5.1 %shard_map.103 = (bf16[128,2048]{1,0:T(8,128)(2,1)S(1)}, bf16[3,128,512]{2,1,0:T(8,128)(2,1)S(1)}, bf16[2,128,512]{2,1,0:T(8,128)(2,1)S(1)}, bf16[4,128,512]{2,1,0:T(8,128)(2,1)S(1)}, bf16[8,128,512]{2,1,0:T(8,128)(2,1)S(1)}) custom-call(s32[6]{0:T(128)S(1)} %stack.94.marks, s32[1,1024]{1,0:T(1,128)S(1)} %bitcast.66, s32[1,1024]{1,0:T(1,128)S(1)} %bitcast.70, ...), custom_call_target="tpu_custom_call" | custom-call | flops 10737418240 | bytes 8388608 | tf_op jit(solution)/shard_map/pallas_call | solution.py:156
  80.4 7.7 %collective-permute-done.19.x_in = bf16[4,128,512]{2,1,0:T(8,128)(2,1)S(1)} collective-permute-done((bf16[4,128,512]{2,1,0:T(8,128)(2,1)S(1)}, bf16[4,128,512]{2,1,0:T(8,128)(2,1)S(1)}, u32[]{:S(2)}, u32[]{:S(2)}) %collective-permute-start.19) | collective-permute-done | bytes 524320 | tf_op jit(solution)/shard_map/ppermute | solution.py:192
  89.6 5.0 %shard_map.104 = (bf16[128,2048]{1,0:T(8,128)(2,1)S(1)}, bf16[3,128,512]{2,1,0:T(8,128)(2,1)S(1)}, bf16[2,128,512]{2,1,0:T(8,128)(2,1)S(1)}, bf16[4,128,512]{2,1,0:T(8,128)(2,1)S(1)}, bf16[8,128,512]{2,1,0:T(8,128)(2,1)S(1)}) custom-call(s32[6]{0:T(128)S(1)} %stack.94.marks, s32[1,1024]{1,0:T(1,128)S(1)} %bitcast.67, s32[1,1024]{1,0:T(1,128)S(1)} %bitcast.71, ...), custom_call_target="tpu_custom_call" | custom-call | flops 10737418240 | bytes 8388608 | tf_op jit(solution)/shard_map/pallas_call | solution.py:156
  98.4 4.9 %collective-permute-done.21 = bf16[4,128,512]{2,1,0:T(8,128)(2,1)S(1)} collective-permute-done((bf16[4,128,512]{2,1,0:T(8,128)(2,1)S(1)}, bf16[4,128,512]{2,1,0:T(8,128)(2,1)S(1)}, u32[]{:S(2)}, u32[]{:S(2)}) %collective-permute-start.21) | collective-permute-done | bytes 524320 | tf_op jit(solution)/shard_map/ppermute | solution.py:192
  103.4 4.7 %collective-permute-start.23 = (bf16[2,128,512]{2,1,0:T(8,128)(2,1)S(1)}, bf16[2,128,512]{2,1,0:T(8,128)(2,1)S(1)}, u32[]{:S(2)}, u32[]{:S(2)}) collective-permute-start(bf16[2,128,512]{2,1,0:T(8,128)(2,1)S(1)} %add_convert_fusion.11), channel_id=1, source_target_pairs={{0,4},{1,5},{2,6},{3,7},{4,0},{5,1},{6,2},{7,3},{8,12},{9,13},{10,... | collective-permute-start | bytes 786440 | tf_op jit(solution)/shard_map/ppermute | solution.py:192
  108.1 5.3 %shard_map.105 = (bf16[128,2048]{1,0:T(8,128)(2,1)S(1)}, bf16[3,128,512]{2,1,0:T(8,128)(2,1)S(1)}, bf16[2,128,512]{2,1,0:T(8,128)(2,1)S(1)}, bf16[4,128,512]{2,1,0:T(8,128)(2,1)S(1)}, bf16[8,128,512]{2,1,0:T(8,128)(2,1)S(1)}) custom-call(s32[6]{0:T(128)S(1)} %stack.94.marks, s32[1,1024]{1,0:T(1,128)S(1)} %bitcast.68, s32[1,1024]{1,0:T(1,128)S(1)} %bitcast.72, ...), custom_call_target="tpu_custom_call" | custom-call | flops 10737418240 | bytes 8388608 | tf_op jit(solution)/shard_map/pallas_call | solution.py:156
  113.6 3.9 %collective-permute-start.31 = (bf16[4,128,512]{2,1,0:T(8,128)(2,1)S(1)}, bf16[4,128,512]{2,1,0:T(8,128)(2,1)S(1)}, u32[]{:S(2)}, u32[]{:S(2)}) collective-permute-start(bf16[4,128,512]{2,1,0:T(8,128)(2,1)S(1)} %add_convert_fusion.1), channel_id=1, source_target_pairs={{0,2},{1,3},{2,0},{3,1},{4,6},{5,7},{6,4},{7,5},{8,10},{9,11},{10,... | collective-permute-start | bytes 1572872 | tf_op jit(solution)/shard_map/ppermute | solution.py:192
  119.1 4.7 %collective-permute-start.27 = (bf16[2,128,512]{2,1,0:T(8,128)(2,1)S(1)}, bf16[2,128,512]{2,1,0:T(8,128)(2,1)S(1)}, u32[]{:S(2)}, u32[]{:S(2)}) collective-permute-start(bf16[2,128,512]{2,1,0:T(8,128)(2,1)S(1)} %add_convert_fusion.10), channel_id=1, source_target_pairs={{0,4},{1,5},{2,6},{3,7},{4,0},{5,1},{6,2},{7,3},{8,12},{9,13},{10,... | collective-permute-start | bytes 786440 | tf_op jit(solution)/shard_map/ppermute | solution.py:192
  123.9 6.2 %collective-permute-done.31 = bf16[4,128,512]{2,1,0:T(8,128)(2,1)S(1)} collective-permute-done((bf16[4,128,512]{2,1,0:T(8,128)(2,1)S(1)}, bf16[4,128,512]{2,1,0:T(8,128)(2,1)S(1)}, u32[]{:S(2)}, u32[]{:S(2)}) %collective-permute-start.31) | collective-permute-done | bytes 524320 | tf_op jit(solution)/shard_map/ppermute | solution.py:192
  130.2 4.7 %collective-permute-start.32 = (bf16[2,128,512]{2,1,0:T(8,128)(2,1)S(1)}, bf16[2,128,512]{2,1,0:T(8,128)(2,1)S(1)}, u32[]{:S(2)}, u32[]{:S(2)}) collective-permute-start(bf16[2,128,512]{2,1,0:T(8,128)(2,1)S(1)} %add_convert_fusion.9), channel_id=1, source_target_pairs={{0,4},{1,5},{2,6},{3,7},{4,0},{5,1},{6,2},{7,3},{8,12},{9,13},{10,... | collective-permute-start | bytes 786440 | tf_op jit(solution)/shard_map/ppermute | solution.py:192
  136.9 4.4 %collective-permute-done.32 = bf16[2,128,512]{2,1,0:T(8,128)(2,1)S(1)} collective-permute-done((bf16[2,128,512]{2,1,0:T(8,128)(2,1)S(1)}, bf16[2,128,512]{2,1,0:T(8,128)(2,1)S(1)}, u32[]{:S(2)}, u32[]{:S(2)}) %collective-permute-start.32) | collective-permute-done | bytes 262176 | tf_op jit(solution)/shard_map/ppermute | solution.py:192
  151.7 30.1 %collective-permute-done.25 = bf16[128,512]{1,0:T(8,128)(2,1)S(1)} collective-permute-done((bf16[128,512]{1,0:T(8,128)(2,1)S(1)}, bf16[128,512]{1,0:T(8,128)(2,1)S(1)}, u32[]{:S(2)}, u32[]{:S(2)}) %collective-permute-start.25) | collective-permute-done | bytes 131104 | tf_op jit(solution)/shard_map/ppermute | solution.py:200
  181.8 9.7 %collective-permute-done.33 = bf16[128,512]{1,0:T(8,128)(2,1)S(1)} collective-permute-done((bf16[128,512]{1,0:T(8,128)(2,1)S(1)}, bf16[128,512]{1,0:T(8,128)(2,1)S(1)}, u32[]{:S(2)}, u32[]{:S(2)}) %collective-permute-start.33) | collective-permute-done | bytes 131104 | tf_op jit(solution)/shard_map/ppermute | solution.py:200
  197.7 5.4 %collective-permute-done.28 = bf16[128,512]{1,0:T(8,128)(2,1)S(1)} collective-permute-done((bf16[128,512]{1,0:T(8,128)(2,1)S(1)}, bf16[128,512]{1,0:T(8,128)(2,1)S(1)}, u32[]{:S(2)}, u32[]{:S(2)}) %collective-permute-start.28) | collective-permute-done | bytes 131104 | tf_op jit(solution)/shard_map/ppermute | solution.py:200
  203.4 8.6 %collective-permute-done.38 = bf16[128,512]{1,0:T(8,128)(2,1)S(1)} collective-permute-done((bf16[128,512]{1,0:T(8,128)(2,1)S(1)}, bf16[128,512]{1,0:T(8,128)(2,1)S(1)}, u32[]{:S(2)}, u32[]{:S(2)}) %collective-permute-start.38) | collective-permute-done | bytes 131104 | tf_op jit(solution)/shard_map/ppermute | solution.py:200
  215.3 5.9 %copy-done = bf16[8192,1024]{1,0:T(8,128)(2,1)S(1)} copy-done((bf16[8192,1024]{1,0:T(8,128)(2,1)S(1)}, bf16[8192,1024]{1,0:T(8,128)(2,1)}, u32[]{:S(2)}) %copy-start) | copy-done | bytes 16777240
  221.3 18.8 %shard_map.106 = bf16[128,8192]{1,0:T(8,128)(2,1)} custom-call(bf16[128,1024]{1,0:T(8,128)(2,1)S(1)} %get-tuple-element.94.key_ref, bf16[128,1024]{1,0:T(8,128)(2,1)S(1)} %get-tuple-element.93.value_ref, bf16[8192,1024]{1,0:T(8,128)(2,1)S(1)} %copy-done, bf16[8192,1024]{1,0:T(8,128)(2,1)} %value_weight_ref.1), custom_call_target="tpu_custom_call" | custom-call | flops 4294967296 | bytes 33554432 | tf_op jit(solution)/shard_map/pallas_call | solution.py:278
  (147 shorter events, 61.7 us)
Async XLA Ops:
  23.6 17.5 %collective-permute-start.3 = (bf16[4,128,512]{2,1,0:T(8,128)(2,1)S(1)}, bf16[4,128,512]{2,1,0:T(8,128)(2,1)S(1)}, u32[]{:S(2)}, u32[]{:S(2)}) collective-permute-start(bf16[4,128,512]{2,1,0:T(8,128)(2,1)S(1)} %pad_maximum_fusion.6), channel_id=1, source_target_pairs={{0,2},{1,3},{2,0},{3,1},{4,6},{5,7},{6,4},{7,5},{8,10},{9,11},{10,... | collective-permute-start | bytes 1572872 | tf_op jit(solution)/shard_map/ppermute | solution.py:192
  25.2 14.3 %collective-permute-start.5 = (bf16[128,512]{1,0:T(8,128)(2,1)S(1)}, bf16[128,512]{1,0:T(8,128)(2,1)S(1)}, u32[]{:S(2)}, u32[]{:S(2)}) collective-permute-start(bf16[128,512]{1,0:T(8,128)(2,1)S(1)} %get-tuple-element.33), channel_id=1, source_target_pairs={{0,16},{1,17},{2,18},{3,19},{4,20},{5,21},{6,22},{7,23},{8,24},{9,... | collective-permute-start | bytes 393224 | tf_op jit(solution)/shard_map/ppermute | solution.py:200
  41.2 24.3 %collective-permute-start.4 = (bf16[8,128,512]{2,1,0:T(8,128)(2,1)S(1)}, bf16[8,128,512]{2,1,0:T(8,128)(2,1)S(1)}, u32[]{:S(2)}, u32[]{:S(2)}) collective-permute-start(bf16[8,128,512]{2,1,0:T(8,128)(2,1)S(1)} %pad_maximum_fusion.1), channel_id=1, source_target_pairs={{0,1},{1,0},{2,3},{3,2},{4,5},{5,4},{6,7},{7,6},{8,9},{9,8},{10,11... | collective-permute-start | bytes 3145736 | tf_op jit(solution)/shard_map/ppermute | solution.py:192
  48.1 17.2 %collective-permute-start.8 = (bf16[4,128,512]{2,1,0:T(8,128)(2,1)S(1)}, bf16[4,128,512]{2,1,0:T(8,128)(2,1)S(1)}, u32[]{:S(2)}, u32[]{:S(2)}) collective-permute-start(bf16[4,128,512]{2,1,0:T(8,128)(2,1)S(1)} %pad_maximum_fusion.7), channel_id=1, source_target_pairs={{0,2},{1,3},{2,0},{3,1},{4,6},{5,7},{6,4},{7,5},{8,10},{9,11},{10,... | collective-permute-start | bytes 1572872 | tf_op jit(solution)/shard_map/ppermute | solution.py:192
  58.6 15.5 %collective-permute-start.18 = (bf16[2,128,512]{2,1,0:T(8,128)(2,1)S(1)}, bf16[2,128,512]{2,1,0:T(8,128)(2,1)S(1)}, u32[]{:S(2)}, u32[]{:S(2)}) collective-permute-start(bf16[2,128,512]{2,1,0:T(8,128)(2,1)S(1)} %get-tuple-element.80), channel_id=1, source_target_pairs={{0,4},{1,5},{2,6},{3,7},{4,0},{5,1},{6,2},{7,3},{8,12},{9,13},{10,... | collective-permute-start | bytes 786440 | tf_op jit(solution)/shard_map/ppermute | solution.py:192
  73.5 16.1 %collective-permute-start.14 = (bf16[8,128,512]{2,1,0:T(8,128)(2,1)S(1)}, bf16[8,128,512]{2,1,0:T(8,128)(2,1)S(1)}, u32[]{:S(2)}, u32[]{:S(2)}) collective-permute-start(bf16[8,128,512]{2,1,0:T(8,128)(2,1)S(1)} %pad_maximum_fusion.3), channel_id=1, source_target_pairs={{0,1},{1,0},{2,3},{3,2},{4,5},{5,4},{6,7},{7,6},{8,9},{9,8},{10,11... | collective-permute-start | bytes 3145736 | tf_op jit(solution)/shard_map/ppermute | solution.py:192
  73.6 14.7 %collective-permute-start.15 = (bf16[8,128,512]{2,1,0:T(8,128)(2,1)S(1)}, bf16[8,128,512]{2,1,0:T(8,128)(2,1)S(1)}, u32[]{:S(2)}, u32[]{:S(2)}) collective-permute-start(bf16[8,128,512]{2,1,0:T(8,128)(2,1)S(1)} %get-tuple-element.40), channel_id=1, source_target_pairs={{0,1},{1,0},{2,3},{3,2},{4,5},{5,4},{6,7},{7,6},{8,9},{9,8},{10,11... | collective-permute-start | bytes 3145736 | tf_op jit(solution)/shard_map/ppermute | solution.py:192
  74.2 14.0 %collective-permute-start.19 = (bf16[4,128,512]{2,1,0:T(8,128)(2,1)S(1)}, bf16[4,128,512]{2,1,0:T(8,128)(2,1)S(1)}, u32[]{:S(2)}, u32[]{:S(2)}) collective-permute-start(bf16[4,128,512]{2,1,0:T(8,128)(2,1)S(1)} %pad_maximum_fusion.9), channel_id=1, source_target_pairs={{0,2},{1,3},{2,0},{3,1},{4,6},{5,7},{6,4},{7,5},{8,10},{9,11},{10,... | collective-permute-start | bytes 1572872 | tf_op jit(solution)/shard_map/ppermute | solution.py:192
  80.4 14.6 %collective-permute-start.22 = (bf16[8,128,512]{2,1,0:T(8,128)(2,1)S(1)}, bf16[8,128,512]{2,1,0:T(8,128)(2,1)S(1)}, u32[]{:S(2)}, u32[]{:S(2)}) collective-permute-start(bf16[8,128,512]{2,1,0:T(8,128)(2,1)S(1)} %get-tuple-element.49), channel_id=1, source_target_pairs={{0,1},{1,0},{2,3},{3,2},{4,5},{5,4},{6,7},{7,6},{8,9},{9,8},{10,11... | collective-permute-start | bytes 3145736 | tf_op jit(solution)/shard_map/ppermute | solution.py:192
  88.2 19.8 %collective-permute-start.20 = (bf16[8,128,512]{2,1,0:T(8,128)(2,1)S(1)}, bf16[8,128,512]{2,1,0:T(8,128)(2,1)S(1)}, u32[]{:S(2)}, u32[]{:S(2)}) collective-permute-start(bf16[8,128,512]{2,1,0:T(8,128)(2,1)S(1)} %pad_maximum_fusion.4), channel_id=1, source_target_pairs={{0,1},{1,0},{2,3},{3,2},{4,5},{5,4},{6,7},{7,6},{8,9},{9,8},{10,11... | collective-permute-start | bytes 3145736 | tf_op jit(solution)/shard_map/ppermute | solution.py:192
  88.5 14.8 %collective-permute-start.21 = (bf16[4,128,512]{2,1,0:T(8,128)(2,1)S(1)}, bf16[4,128,512]{2,1,0:T(8,128)(2,1)S(1)}, u32[]{:S(2)}, u32[]{:S(2)}) collective-permute-start(bf16[4,128,512]{2,1,0:T(8,128)(2,1)S(1)} %add_convert_fusion.3), channel_id=1, source_target_pairs={{0,2},{1,3},{2,0},{3,1},{4,6},{5,7},{6,4},{7,5},{8,10},{9,11},{10,... | collective-permute-start | bytes 1572872 | tf_op jit(solution)/shard_map/ppermute | solution.py:192
  94.7 18.7 %collective-permute-start.30 = (bf16[8,128,512]{2,1,0:T(8,128)(2,1)S(1)}, bf16[8,128,512]{2,1,0:T(8,128)(2,1)S(1)}, u32[]{:S(2)}, u32[]{:S(2)}) collective-permute-start(bf16[8,128,512]{2,1,0:T(8,128)(2,1)S(1)} %get-tuple-element.53), channel_id=1, source_target_pairs={{0,1},{1,0},{2,3},{3,2},{4,5},{5,4},{6,7},{7,6},{8,9},{9,8},{10,11... | collective-permute-start | bytes 3145736 | tf_op jit(solution)/shard_map/ppermute | solution.py:192
  95.1 23.9 %collective-permute-start.26 = (bf16[4,128,512]{2,1,0:T(8,128)(2,1)S(1)}, bf16[4,128,512]{2,1,0:T(8,128)(2,1)S(1)}, u32[]{:S(2)}, u32[]{:S(2)}) collective-permute-start(bf16[4,128,512]{2,1,0:T(8,128)(2,1)S(1)} %add_convert_fusion.2), channel_id=1, source_target_pairs={{0,2},{1,3},{2,0},{3,1},{4,6},{5,7},{6,4},{7,5},{8,10},{9,11},{10,... | collective-permute-start | bytes 1572872 | tf_op jit(solution)/shard_map/ppermute | solution.py:192
  103.4 33.5 %collective-permute-start.23 = (bf16[2,128,512]{2,1,0:T(8,128)(2,1)S(1)}, bf16[2,128,512]{2,1,0:T(8,128)(2,1)S(1)}, u32[]{:S(2)}, u32[]{:S(2)}) collective-permute-start(bf16[2,128,512]{2,1,0:T(8,128)(2,1)S(1)} %add_convert_fusion.11), channel_id=1, source_target_pairs={{0,4},{1,5},{2,6},{3,7},{4,0},{5,1},{6,2},{7,3},{8,12},{9,13},{10,... | collective-permute-start | bytes 786440 | tf_op jit(solution)/shard_map/ppermute | solution.py:192
  113.4 21.5 %collective-permute-start.35 = (bf16[8,128,512]{2,1,0:T(8,128)(2,1)S(1)}, bf16[8,128,512]{2,1,0:T(8,128)(2,1)S(1)}, u32[]{:S(2)}, u32[]{:S(2)}) collective-permute-start(bf16[8,128,512]{2,1,0:T(8,128)(2,1)S(1)} %get-tuple-element.57), channel_id=1, source_target_pairs={{0,1},{1,0},{2,3},{3,2},{4,5},{5,4},{6,7},{7,6},{8,9},{9,8},{10,11... | collective-permute-start | bytes 3145736 | tf_op jit(solution)/shard_map/ppermute | solution.py:192
  113.6 16.5 %collective-permute-start.31 = (bf16[4,128,512]{2,1,0:T(8,128)(2,1)S(1)}, bf16[4,128,512]{2,1,0:T(8,128)(2,1)S(1)}, u32[]{:S(2)}, u32[]{:S(2)}) collective-permute-start(bf16[4,128,512]{2,1,0:T(8,128)(2,1)S(1)} %add_convert_fusion.1), channel_id=1, source_target_pairs={{0,2},{1,3},{2,0},{3,1},{4,6},{5,7},{6,4},{7,5},{8,10},{9,11},{10,... | collective-permute-start | bytes 1572872 | tf_op jit(solution)/shard_map/ppermute | solution.py:192
  119.1 72.5 %collective-permute-start.27 = (bf16[2,128,512]{2,1,0:T(8,128)(2,1)S(1)}, bf16[2,128,512]{2,1,0:T(8,128)(2,1)S(1)}, u32[]{:S(2)}, u32[]{:S(2)}) collective-permute-start(bf16[2,128,512]{2,1,0:T(8,128)(2,1)S(1)} %add_convert_fusion.10), channel_id=1, source_target_pairs={{0,4},{1,5},{2,6},{3,7},{4,0},{5,1},{6,2},{7,3},{8,12},{9,13},{10,... | collective-permute-start | bytes 786440 | tf_op jit(solution)/shard_map/ppermute | solution.py:192
  135.0 13.5 %collective-permute-start.36 = (bf16[4,128,512]{2,1,0:T(8,128)(2,1)S(1)}, bf16[4,128,512]{2,1,0:T(8,128)(2,1)S(1)}, u32[]{:S(2)}, u32[]{:S(2)}) collective-permute-start(bf16[4,128,512]{2,1,0:T(8,128)(2,1)S(1)} %add_convert_fusion), channel_id=1, source_target_pairs={{0,2},{1,3},{2,0},{3,1},{4,6},{5,7},{6,4},{7,5},{8,10},{9,11},{10,... | collective-permute-start | bytes 1572872 | tf_op jit(solution)/shard_map/ppermute | solution.py:192
  143.5 38.3 %collective-permute-start.25 = (bf16[128,512]{1,0:T(8,128)(2,1)S(1)}, bf16[128,512]{1,0:T(8,128)(2,1)S(1)}, u32[]{:S(2)}, u32[]{:S(2)}) collective-permute-start(bf16[128,512]{1,0:T(8,128)(2,1)S(1)} %get-tuple-element.68), channel_id=1, source_target_pairs={{8,0},{9,1},{10,2},{11,3},{12,4},{13,5},{14,6},{15,7},{16,8},{17,9... | collective-permute-start | bytes 393224 | tf_op jit(solution)/shard_map/ppermute | solution.py:200
  144.8 46.7 %collective-permute-start.33 = (bf16[128,512]{1,0:T(8,128)(2,1)S(1)}, bf16[128,512]{1,0:T(8,128)(2,1)S(1)}, u32[]{:S(2)}, u32[]{:S(2)}) collective-permute-start(bf16[128,512]{1,0:T(8,128)(2,1)S(1)} %get-tuple-element.71), channel_id=1, source_target_pairs={{16,0},{17,1},{18,2},{19,3},{20,4},{21,5},{22,6},{23,7},{24,8},{25... | collective-permute-start | bytes 393224 | tf_op jit(solution)/shard_map/ppermute | solution.py:200
  148.6 43.0 %collective-permute-start.34 = (bf16[128,512]{1,0:T(8,128)(2,1)S(1)}, bf16[128,512]{1,0:T(8,128)(2,1)S(1)}, u32[]{:S(2)}, u32[]{:S(2)}) collective-permute-start(bf16[128,512]{1,0:T(8,128)(2,1)S(1)} %get-tuple-element.72), channel_id=1, source_target_pairs={{8,0},{9,1},{10,2},{11,3},{12,4},{13,5},{14,6},{15,7},{16,8},{17,9... | collective-permute-start | bytes 393224 | tf_op jit(solution)/shard_map/ppermute | solution.py:200
  150.0 41.6 %collective-permute-start.37 = (bf16[2,128,512]{2,1,0:T(8,128)(2,1)S(1)}, bf16[2,128,512]{2,1,0:T(8,128)(2,1)S(1)}, u32[]{:S(2)}, u32[]{:S(2)}) collective-permute-start(bf16[2,128,512]{2,1,0:T(8,128)(2,1)S(1)} %add_convert_fusion.8), channel_id=1, source_target_pairs={{0,4},{1,5},{2,6},{3,7},{4,0},{5,1},{6,2},{7,3},{8,12},{9,13},{10,... | collective-permute-start | bytes 786440 | tf_op jit(solution)/shard_map/ppermute | solution.py:192
  195.1 16.8 %collective-permute-start.38 = (bf16[128,512]{1,0:T(8,128)(2,1)S(1)}, bf16[128,512]{1,0:T(8,128)(2,1)S(1)}, u32[]{:S(2)}, u32[]{:S(2)}) collective-permute-start(bf16[128,512]{1,0:T(8,128)(2,1)S(1)} %get-tuple-element.73), channel_id=1, source_target_pairs={{16,0},{17,1},{18,2},{19,3},{20,4},{21,5},{22,6},{23,7},{24,8},{25... | collective-permute-start | bytes 393224 | tf_op jit(solution)/shard_map/ppermute | solution.py:200
  196.4 15.5 %collective-permute-start.39 = (bf16[128,512]{1,0:T(8,128)(2,1)S(1)}, bf16[128,512]{1,0:T(8,128)(2,1)S(1)}, u32[]{:S(2)}, u32[]{:S(2)}) collective-permute-start(bf16[128,512]{1,0:T(8,128)(2,1)S(1)} %get-tuple-element.74), channel_id=1, source_target_pairs={{8,0},{9,1},{10,2},{11,3},{12,4},{13,5},{14,6},{15,7},{16,8},{17,9... | collective-permute-start | bytes 393224 | tf_op jit(solution)/shard_map/ppermute | solution.py:200
  (32 other events, 529.4 us)
